TPU v7x, 512 devices: a whole 4x4x16 slice. The times are simulated.
512 devices in a mesh: row: 32 (over z, x_hi), col: 16 (over x_lo, y, core).
Axes of the slice: x: 4 (x_hi: 2, x_lo: 2; x = x_hi * 2 + x_lo), y: 4, z: 16, core: 2. Of those that a mesh axis runs over, the one named last changes fastest.
Arguments:
- activations: bfloat16 [1024, 5120], P('row'), may hold values from -6 to 6
- act_basis: bfloat16 [5120, 5120], P('row', 'col'), may hold values from -0.078125 to 0.078125
- gradients: bfloat16 [1024, 27648], P('row', 'col'), may hold values from -6 to 6
- grad_basis: bfloat16 [27648, 27648], P('col', 'row'), may hold values from -0.0390625 to 0.0390625
Outputs:
- correction: float32 [5120, 27648], P('col', 'row')
All inputs are finite; a program needn't handle non-finite values.
Results may differ from a plain program's by a relative error of at most 0.0041.
Values may be sent and summed in bfloat16 or wider, within the bound.
No kernel may reach another device: no remote copies, remote signals or barrier semaphores. Data moves between devices by JAX's collectives and lax.ppermute only.
A program may use at most 64 MiB of HBM per device.

v0:
```python
import jax
import jax.numpy as jnp
from jax import lax
from jax.sharding import PartitionSpec as P

SEQ_LEN = 512
SEQS = 2


def local(activations, act_basis, gradients, grad_basis):
    rotated_own = jnp.dot(
        activations,
        lax.all_gather(act_basis, "row", axis=0, tiled=True),
        preferred_element_type=jnp.float32,
    ).astype(jnp.bfloat16)
    rotated_acts = lax.all_gather(rotated_own, "row", axis=0, tiled=True)
    partial_grads = jnp.dot(
        lax.all_gather(gradients, "row", axis=0, tiled=True),
        grad_basis,
        preferred_element_type=jnp.float32,
    )
    rotated_grads = lax.psum(partial_grads, "col").astype(jnp.bfloat16)
    total = jnp.zeros((rotated_acts.shape[1], rotated_grads.shape[1]), jnp.float32)
    for seq_index in range(SEQS):
        acts_seq = rotated_acts[seq_index * SEQ_LEN : (seq_index + 1) * SEQ_LEN]
        grads_seq = rotated_grads[seq_index * SEQ_LEN : (seq_index + 1) * SEQ_LEN]
        seq_grad = lax.dot_general(
            acts_seq, grads_seq, (((0,), (0,)), ((), ())), preferred_element_type=jnp.float32
        )
        total = total + seq_grad * seq_grad
    return total / (SEQS * SEQ_LEN)


def solution(mesh):
    return jax.shard_map(
        local,
        mesh=mesh,
        in_specs=(P("row", None), P("row", "col"), P("row", "col"), P("col", "row")),
        out_specs=P("col", "row"),
        check_vma=False,
    )
```

profile of v0, /device:TPU:1, one launch (start us, length us, event | category | flops | bytes accessed | tf_op | source)
XLA Modules:
  0.0 421.0 jit_solution(9495876810830057809)
XLA Ops:
  6.5 0.0 copy-start
  6.5 0.0 all-gather.3.cloned.1.call-start
  6.5 0.7 all-gather.3.cloned.1.call-update
  7.3 0.0 all-gather.5.cloned.1.call-start
  7.3 0.7 all-gather.5.cloned.1.call-update
  8.0 162.4 %all-gather.3.cloned.1.call-done = bf16[5120,320]{1,0:T(8,128)(2,1)} async-done(((bf16[160,320]{1,0:T(8,128)(2,1)}), bf16[5120,320]{1,0:T(8,128)(2,1)}) %all-gather.3.cloned.1.call-update) | async-done | bytes 3276816 | tf_op jit(solution)/shard_map/all_gather | solution.py:13
  170.4 2.9 convolution_convert_fusion
  173.3 67.8 %all_gather.10 = bf16[1024,320]{1,0:T(8,128)(2,1)} all-gather(bf16[32,320]{1,0:T(8,128)(2,1)S(1)} %convolution_convert_fusion), channel_id=1, replica_groups=mesh['row'=32,'col'=16] {'row'}, dimensions={0}, use_global_device_ids=true | all-gather | bytes 675840 | tf_op jit(solution)/shard_map/all_gather | solution.py:16
  241.1 86.5 %all-gather.5.cloned.1.call-done = bf16[1024,1728]{1,0:T(8,128)(2,1)} async-done(((bf16[32,1728]{1,0:T(8,128)(2,1)}), bf16[1024,1728]{1,0:T(8,128)(2,1)}) %all-gather.5.cloned.1.call-update) | async-done | bytes 3538960 | tf_op jit(solution)/shard_map/all_gather | solution.py:18
  327.6 0.0 copy-done
  327.6 7.2 %fusion.6 = f32[1024,864]{0,1:T(8,128)} fusion(bf16[1024,1728]{1,0:T(8,128)(2,1)} %all-gather.5.cloned.1.call-done, bf16[1728,864]{1,0:T(8,128)(2,1)S(1)} %copy-done), kind=kOutput, calls=%fused_computation.9 | convolution fusion | flops 3057647616 | bytes 10063872 | tf_op jit(solution)/shard_map/dot_general | solution.py:17
  334.8 74.7 %all-reduce.1 = bf16[1024,864]{0,1:T(8,128)(2,1)} all-reduce(f32[1024,864]{0,1:T(8,128)} %fusion.6), channel_id=1, replica_groups=mesh['row'=32,'col'=16] {'col'}, use_global_device_ids=true, to_apply=%region_0.0 | all-reduce | flops 884736 | bytes 5308416 | tf_op jit(solution)/shard_map/psum | solution.py:22
  409.6 0.0 copy-start.1
  409.6 2.0 convolution_multiply_fusion
  411.6 0.0 copy-done.1
  411.6 2.6 fusion.1
Async XLA Ops:
  6.5 321.1 %copy-start = (bf16[1728,864]{1,0:T(8,128)(2,1)S(1)}, bf16[1728,864]{1,0:T(8,128)(2,1)}, u32[]{:S(2)}) copy-start(bf16[1728,864]{1,0:T(8,128)(2,1)} %param.7) | copy-start | bytes 8957956
  6.5 163.9 %all-gather.3.cloned.1.call-start = ((), (), s32[]{:S(2)}) async-start(), calls=%async_computation | async-start | bytes 4055040 | tf_op jit(solution)/shard_map/all_gather | solution.py:13
  7.3 320.3 %all-gather.5.cloned.1.call-start = ((), (), s32[]{:S(2)}) async-start(), calls=%async_computation.1 | async-start | bytes 3784704 | tf_op jit(solution)/shard_map/all_gather | solution.py:18
  409.6 2.0 copy-start.1
Sparse Core Ops, SparseCore 0:
  10.5 159.8 all-gather.2
  173.5 154.0 all-gather.4
where the time goes:
time: 424 us; the launch traced here: 421 us
  waiting for transfers between devices  250 us (59%)
  blocking collectives  143 us (34%)
  matrix products  14.7 us (3%)
  between operations  13.4 us (3%)
    all_gather x1, waiting for transfers between devices, local(): lax.all_gather(act_basis, 'row', axis=0, tiled=True)  162 us
    all_gather x1, waiting for transfers between devices, local(): lax.all_gather(gradients, 'row', axis=0, tiled=True)  86.5 us
    psum x1, blocking collectives, local(): rotated_grads = lax.psum(partial_grads, 'col').astype(jnp.bfloat16)  74.7 us
    all_gather x1, blocking collectives, local(): rotated_acts = lax.all_gather(rotated_own, 'row', axis=0, tiled=True)  67.8 us
  transfers between devices with their start and end apart: 2, of which 2 were waited for; matrix products, arithmetic and copies ran while one was open for 1% of the time, Pallas kernels for 0%

commit v1 on v0

v1 whole, which is shorter than its diff:
```python
import jax
import jax.numpy as jnp
from jax import lax
from jax.sharding import Mesh
from jax.sharding import PartitionSpec as P

SEQ_LEN = 512
SEQS = 2
NZ, NXH, NXL, NY, NCORE = 16, 2, 2, 4, 2
ROW = ("z", "xh")
COL = ("xl", "y", "core")
SWAP = [(0, 1), (1, 0)]
BF, F32 = jnp.bfloat16, jnp.float32

PARITY = [[p + 2 * k for k in range(NZ // 2)] for p in range(2)]
QUADS = [[(2 * k + i) * NXH + h for i in range(2) for h in range(NXH)] for k in range(NZ // 2)]


def dot(a, b):
    return jnp.dot(a, b, preferred_element_type=F32)


def dot_t(a, b):
    return lax.dot_general(a, b, (((0,), (0,)), ((), ())), preferred_element_type=F32)


def total(x):
    out = x[0].astype(F32)
    for i in range(1, x.shape[0]):
        out = out + x[i].astype(F32)
    return out


def rotate_acts(activations, act_basis):
    tokens, width = activations.shape
    block, cols = act_basis.shape
    parts = activations.reshape(tokens, NZ // 2, 4, block).transpose(2, 0, 1, 3)
    parts = parts.reshape(4, tokens, width // 4)
    parts = lax.all_to_all(parts, ROW, 0, 0, axis_index_groups=QUADS)
    basis = lax.all_gather(act_basis, "z", axis=0, tiled=True, axis_index_groups=PARITY)
    partial = dot(parts.reshape(4 * tokens, width // 4), basis)
    partial = jnp.broadcast_to(
        partial.reshape(2, 1, 2 * tokens, cols), (2, 2, 2 * tokens, cols)
    ).reshape(4, 2 * tokens, cols)
    partial = lax.all_to_all(partial, ROW, 0, 0, axis_index_groups=QUADS)
    rotated = total(partial).astype(BF)
    return lax.all_gather(rotated, "z", axis=0, tiled=True)


def local(activations, act_basis, gradients, grad_basis):
    core = lax.axis_index("core")
    xh = lax.axis_index("xh")
    other = lax.ppermute(gradients, "xh", SWAP)
    pair = jnp.where(
        xh == 0,
        jnp.concatenate([gradients, other]),
        jnp.concatenate([other, gradients]),
    )
    grads = lax.all_gather(pair, "z", axis=0, tiled=True)
    rotated_acts = rotate_acts(activations, act_basis)
    grads, rotated_acts = lax.optimization_barrier((grads, rotated_acts))

    def half(x, index):
        return lax.dynamic_slice_in_dim(x, index * SEQ_LEN, SEQ_LEN, 0)

    theirs = lax.ppermute(dot(half(grads, 1 - core), grad_basis), "core", SWAP)
    partial = (dot(half(grads, core), grad_basis) + theirs).astype(BF)
    n = NXL * NY
    cols = partial.shape[1]
    partial = lax.all_to_all(partial.reshape(n, SEQ_LEN // n, cols), ("xl", "y"), 0, 0)
    own = total(partial).astype(BF)
    own = lax.all_to_all(jnp.broadcast_to(own[None], (n,) + own.shape), ("xl", "y"), 0, 0)
    own = own.reshape(SEQ_LEN, cols)
    rest = lax.ppermute(own, "core", SWAP)
    first = dot_t(half(rotated_acts, core), own)
    second = dot_t(half(rotated_acts, 1 - core), rest)
    return (first * first + second * second) / (SEQS * SEQ_LEN)


def solution(mesh):
    split = Mesh(
        mesh.devices.reshape(NZ, NXH, NXL, NY, NCORE), ("z", "xh", "xl", "y", "core")
    )
    return jax.shard_map(
        local,
        mesh=split,
        in_specs=(P(ROW, None), P(ROW, COL), P(ROW, COL), P(COL, ROW)),
        out_specs=P(COL, ROW),
        check_vma=False,
    )
```

time: 424 us -> 200 us (0.47)
  waiting for transfers between devices: 250 us -> 14.5 us
  starting transfers between devices: 0.04 us -> 36.3 us
  blocking collectives: 143 us -> 107 us
  local copies, waits for them, and re-layouts: 0.01 us -> 11.9 us
    all_gather x2 -> x1, waiting for transfers between devices: 249 us -> 0.01 us  [local(): grads = lax.all_gather(pair, 'z', axis=0, tiled=True)]
    psum x1 -> x0, blocking collectives: 74.7 us -> none  [local(): rotated_grads = lax.psum(partial_grads, 'col').astype(jnp.bfloat16)]
    all_to_all x0 -> x2, blocking collectives: none -> 33.4 us  [the longest x1 18.2 us: local(): lax.all_to_all(partial.reshape(n, SEQ_LEN // n, cols), ('xl', 'y'), 0, 0)]
    ppermute x0 -> x3, starting transfers between devices: none -> 24 us  [the longest x1 13.1 us: local(): theirs = lax.ppermute(dot(half(grads, 1 - core), grad_basis), 'core', SWAP)]
    all_to_all x0 -> x2, starting transfers between devices: none -> 12.3 us  [the longest x1 6.39 us: rotate_acts(): partial = lax.all_to_all(partial, ROW, 0, 0, axis_index_groups=QUADS)]
    all_to_all x0 -> x2, waiting for transfers between devices: none -> 8.05 us  [the longest x1 8.05 us: rotate_acts(): partial = lax.all_to_all(partial, ROW, 0, 0, axis_index_groups=QUADS)]
    reshape x0 -> x3, local copies, waits for them, and re-layouts: none -> 6.85 us  [the longest x1 2.36 us: rotate_acts(): parts = activations.reshape(tokens, NZ // 2, 4, block).transpose(2, 0, 1, 3)]
    ppermute x0 -> x3, waiting for transfers between devices: none -> 6.4 us  [the longest x1 3.63 us: local(): theirs = lax.ppermute(dot(half(grads, 1 - core), grad_basis), 'core', SWAP)]
  transfers between devices with their start and end apart: 2 -> 6, of which waited for: 2 -> 4; matrix products, arithmetic and copies ran while one was open for 1% -> 5% of each run, Pallas kernels for 0% -> 0%
where the time goes in v1:
time: 200 us; the launch traced here: 199 us
  blocking collectives  107 us (54%)
  starting transfers between devices  36.3 us (18%)
  waiting for transfers between devices  14.5 us (7%)
  matrix products  14.3 us (7%)
  between operations  13.5 us (7%)
  local copies, waits for them, and re-layouts  11.9 us (6%)
    all_gather x1, blocking collectives, rotate_acts(): lax.all_gather(act_basis, 'z', axis=0, tiled=True, axis_index_groups=PARITY)  39.5 us
    all_gather x1, blocking collectives, rotate_acts(): return lax.all_gather(rotated, 'z', axis=0, tiled=True)  33.7 us
    all_to_all x1, blocking collectives, local(): lax.all_to_all(partial.reshape(n, SEQ_LEN // n, cols), ('xl', 'y'), 0, 0)  18.2 us
    all_to_all x1, blocking collectives, local(): lax.all_to_all(jnp.broadcast_to(own[None], (n,) + own.shape), ('xl', 'y')...  15.2 us
    ppermute x1, starting transfers between devices, local(): theirs = lax.ppermute(dot(half(grads, 1 - core), grad_basis), 'core', SWAP)  13.1 us
    dot_general x3, matrix products, dot(): return jnp.dot(a, b, preferred_element_type=F32)  10.9 us
    all_to_all x1, waiting for transfers between devices, rotate_acts(): partial = lax.all_to_all(partial, ROW, 0, 0, axis_index_groups=QUADS)  8.05 us
    all_to_all x1, starting transfers between devices, rotate_acts(): partial = lax.all_to_all(partial, ROW, 0, 0, axis_index_groups=QUADS)  6.39 us
  transfers between devices with their start and end apart: 6, of which 4 were waited for; matrix products, arithmetic and copies ran while one was open for 5% of the time, Pallas kernels for 0%

profile of v1, /device:TPU:1, one launch (start us, length us, event | category | flops | bytes accessed | tf_op | source)
XLA Modules:
  0.0 198.9 jit_solution(5953931089574811103)
XLA Ops:
  6.5 5.7 %collective-permute-start = (bf16[32,1728]{1,0:T(8,128)(2,1)}, bf16[32,1728]{1,0:T(8,128)(2,1)S(1)}, u32[]{:S(2)}, u32[]{:S(2)}) collective-permute-start(bf16[32,1728]{1,0:T(8,128)(2,1)} %param.6), channel_id=1, source_target_pairs={{0,16},{16,0},{1,17},{17,1},{2,18},{18,2},{3,19},{19,3},{4,20},{20... | collective-permute-start | bytes 331784 | tf_op jit(solution)/shard_map/ppermute | solution.py:53
  12.3 2.4 %collective-permute-done = bf16[32,1728]{1,0:T(8,128)(2,1)S(1)} collective-permute-done((bf16[32,1728]{1,0:T(8,128)(2,1)}, bf16[32,1728]{1,0:T(8,128)(2,1)S(1)}, u32[]{:S(2)}, u32[]{:S(2)}) %collective-permute-start) | collective-permute-done | bytes 110624 | tf_op jit(solution)/shard_map/ppermute | solution.py:53
  14.7 1.7 maximum_select_fusion
  16.4 2.4 %reshape.29 = bf16[32,8,4,160]{3,2,1,0:T(4,128)(2,1)} reshape(bf16[32,5120]{1,0:T(8,128)(2,1)} %param.4) | data formatting | bytes 655360 | tf_op jit(solution)/shard_map/reshape | solution.py:37
  18.8 1.9 copy.12
  20.7 2.3 %reshape.30 = bf16[4,32,1280]{2,1,0:T(8,128)(2,1)} reshape(bf16[4,32,8,160]{3,2,1,0:T(8,128)(2,1)} %copy.12) | data formatting | bytes 655360 | tf_op jit(solution)/shard_map/reshape | solution.py:38
  23.0 6.0 %all-to-all-start = ((bf16[4,32,1280]{2,1,0:T(8,128)(2,1)}), bf16[4,32,1280]{2,1,0:T(8,128)(2,1)S(1)}, u32[]{:S(2)}, u32[]{:S(2)}) async-start(bf16[4,32,1280]{2,1,0:T(8,128)(2,1)} %reshape.30), calls=%async_computation | async-start | bytes 655360 | tf_op jit(solution)/shard_map/all_to_all | solution.py:39
  28.9 39.5 %all_gather.10 = bf16[1280,320]{1,0:T(8,128)(2,1)} all-gather(bf16[160,320]{1,0:T(8,128)(2,1)S(1)} %copy-done.2), channel_id=1, replica_groups={{0,64,128,192,256,320,384,448},{32,96,160,224,288,352,416,480},{1,65,12..., dimensions={0}, use_global_device_ids=true | all-gather | bytes 921600 | tf_op jit(solution)/shard_map/all_gather | solution.py:40
  68.4 1.5 fusion.8
  70.0 0.8 broadcast_in_dim.6
  70.8 6.4 %all-to-all-start.1 = ((f32[4,64,320]{2,1,0:T(8,128)}), f32[4,64,320]{2,1,0:T(8,128)S(1)}, u32[]{:S(2)}, u32[]{:S(2)}) async-start(f32[4,64,320]{2,1,0:T(8,128)} %bitcast.24), calls=%async_computation.1 | async-start | bytes 786432 | tf_op jit(solution)/shard_map/all_to_all | solution.py:45
  77.1 8.1 %all-to-all-done.1 = f32[4,64,320]{2,1,0:T(8,128)S(1)} async-done(((f32[4,64,320]{2,1,0:T(8,128)}), f32[4,64,320]{2,1,0:T(8,128)S(1)}, u32[]{:S(2)}, u32[]{:S(2)}) %all-to-all-start.1) | async-done | bytes 327712 | tf_op jit(solution)/shard_map/all_to_all | solution.py:45
  85.2 33.7 %all-gather = bf16[1,1024,320]{2,1,0:T(8,128)(2,1)} all-gather(bf16[1,64,320]{2,1,0:T(8,128)(2,1)S(1)} %fusion.13), channel_id=2, replica_groups=mesh['z'=16,'xh'=2,'xl'=2,'y'=4,'core'=2] {'z'}, dimensions={1}, use_global_device_ids=true | all-gather | bytes 696320 | tf_op jit(solution)/shard_map/all_gather | solution.py:47
  118.9 4.6 %fusion = f32[512,864]{0,1:T(8,128)} fusion(bf16[1728,864]{1,0:T(8,128)(2,1)S(1)} %copy-done, bf16[1024,1728]{1,0:T(8,128)(2,1)} %all-gather.3.cloned.1.call-done, s32[]{:T(128)S(6)} %select_n.19), kind=kOutput, calls=%fused_computation | convolution fusion | flops 1528823808 | bytes 6590468 | tf_op jit(solution)/shard_map/dot_general | solution.py:20
  123.5 13.1 %collective-permute-start.1 = (f32[512,864]{0,1:T(8,128)}, f32[512,864]{0,1:T(8,128)}, u32[]{:S(2)}, u32[]{:S(2)}) collective-permute-start(f32[512,864]{0,1:T(8,128)} %fusion), channel_id=1, source_target_pairs={{0,1},{1,0},{2,3},{3,2},{4,5},{5,4},{6,7},{7,6},{8,9},{9,8},{10,11... | collective-permute-start | bytes 5308424 | tf_op jit(solution)/shard_map/ppermute | solution.py:66
  136.6 3.6 %collective-permute-done.1 = f32[512,864]{0,1:T(8,128)} collective-permute-done((f32[512,864]{0,1:T(8,128)}, f32[512,864]{0,1:T(8,128)}, u32[]{:S(2)}, u32[]{:S(2)}) %collective-permute-start.1) | collective-permute-done | bytes 1769504 | tf_op jit(solution)/shard_map/ppermute | solution.py:66
  140.2 4.8 %add_convert_fusion = bf16[512,864]{0,1:T(8,128)(2,1)} fusion(f32[512,864]{0,1:T(8,128)} %collective-permute-done.1, bf16[1728,864]{1,0:T(8,128)(2,1)S(1)} %copy-done, bf16[1024,1728]{1,0:T(8,128)(2,1)} %all-gather.3.cloned.1.call-done, s32[]{:T(128)S(6)} %select_n.18), kind=kOutput, calls=%fused_computation.4 | convolution fusion | flops 1529708544 | bytes 7475204 | tf_op jit(solution)/shard_map/dot_general | solution.py:20
  145.0 2.2 %copy.13 = bf16[512,864]{1,0:T(8,128)(2,1)} copy(bf16[512,864]{0,1:T(8,128)(2,1)} %add_convert_fusion) | data formatting | bytes 1769472 | tf_op jit(solution)/shard_map/convert_element_type | solution.py:67
  147.2 18.2 %all_to_all.20 = bf16[8,64,864]{2,1,0:T(8,128)(2,1)S(1)} all-to-all(bf16[8,64,864]{2,1,0:T(8,128)(2,1)} %bitcast.20), channel_id=1, replica_groups=mesh['z'=16,'xh'=2,'xl'=2,'y'=4,'core'=2] {'xl','y'}, dimensions={0} | all-to-all | bytes 1769472 | tf_op jit(solution)/shard_map/all_to_all | solution.py:70
  165.7 15.2 %all_to_all.21 = bf16[8,64,864]{2,1,0:T(8,128)(2,1)} all-to-all(bf16[8,64,864]{2,1,0:T(8,128)(2,1)S(1)} %broadcast_in_dim.15), channel_id=1, replica_groups=mesh['z'=16,'xh'=2,'xl'=2,'y'=4,'core'=2] {'xl','y'}, dimensions={0} | all-to-all | bytes 1769472 | tf_op jit(solution)/shard_map/all_to_all | solution.py:72
  180.9 2.2 %copy.14 = bf16[512,864]{0,1:T(8,128)(2,1)} copy(bf16[512,864]{1,0:T(8,128)(2,1)} %bitcast.18) | data formatting | bytes 1769472 | tf_op jit(solution)/shard_map/reshape | solution.py:73
  183.1 5.2 %collective-permute-start.2 = (bf16[512,864]{0,1:T(8,128)(2,1)}, bf16[512,864]{0,1:T(8,128)(2,1)S(1)}, u32[]{:S(2)}, u32[]{:S(2)}) collective-permute-start(bf16[512,864]{0,1:T(8,128)(2,1)} %copy.14), channel_id=1, source_target_pairs={{0,1},{1,0},{2,3},{3,2},{4,5},{5,4},{6,7},{7,6},{8,9},{9,8},{10,11... | collective-permute-start | bytes 2654216 | tf_op jit(solution)/shard_map/ppermute | solution.py:74
  188.2 1.8 convolution_multiply_fusion.1
  190.5 1.6 fusion.7
  (14 shorter events, 0.7 us)
Async XLA Ops:
  6.5 112.4 %copy-start = (bf16[1728,864]{1,0:T(8,128)(2,1)S(1)}, bf16[1728,864]{1,0:T(8,128)(2,1)}, u32[]{:S(2)}) copy-start(bf16[1728,864]{1,0:T(8,128)(2,1)} %param.7) | copy-start | bytes 8957956
  6.5 112.4 %all-gather.3.cloned.1.call-start = ((), (), s32[]{:S(2)}) async-start(), calls=%async_computation.4 | async-start | bytes 3899392 | tf_op jit(solution)/shard_map/all_gather | solution.py:59
  6.5 8.1 %collective-permute-start = (bf16[32,1728]{1,0:T(8,128)(2,1)}, bf16[32,1728]{1,0:T(8,128)(2,1)S(1)}, u32[]{:S(2)}, u32[]{:S(2)}) collective-permute-start(bf16[32,1728]{1,0:T(8,128)(2,1)} %param.6), channel_id=1, source_target_pairs={{0,16},{16,0},{1,17},{17,1},{2,18},{18,2},{3,19},{19,3},{4,20},{20... | collective-permute-start | bytes 331784 | tf_op jit(solution)/shard_map/ppermute | solution.py:53
  16.4 12.5 %copy-start.2 = (bf16[160,320]{1,0:T(8,128)(2,1)S(1)}, bf16[160,320]{1,0:T(8,128)(2,1)}, u32[]{:S(2)}) copy-start(bf16[160,320]{1,0:T(8,128)(2,1)} %param.5) | copy-start | bytes 307204
  23.0 45.4 %all-to-all-start = ((bf16[4,32,1280]{2,1,0:T(8,128)(2,1)}), bf16[4,32,1280]{2,1,0:T(8,128)(2,1)S(1)}, u32[]{:S(2)}, u32[]{:S(2)}) async-start(bf16[4,32,1280]{2,1,0:T(8,128)(2,1)} %reshape.30), calls=%async_computation | async-start | bytes 655360 | tf_op jit(solution)/shard_map/all_to_all | solution.py:39
  70.8 14.4 %all-to-all-start.1 = ((f32[4,64,320]{2,1,0:T(8,128)}), f32[4,64,320]{2,1,0:T(8,128)S(1)}, u32[]{:S(2)}, u32[]{:S(2)}) async-start(f32[4,64,320]{2,1,0:T(8,128)} %bitcast.24), calls=%async_computation.1 | async-start | bytes 786432 | tf_op jit(solution)/shard_map/all_to_all | solution.py:45
  123.5 16.7 %collective-permute-start.1 = (f32[512,864]{0,1:T(8,128)}, f32[512,864]{0,1:T(8,128)}, u32[]{:S(2)}, u32[]{:S(2)}) collective-permute-start(f32[512,864]{0,1:T(8,128)} %fusion), channel_id=1, source_target_pairs={{0,1},{1,0},{2,3},{3,2},{4,5},{5,4},{6,7},{7,6},{8,9},{9,8},{10,11... | collective-permute-start | bytes 5308424 | tf_op jit(solution)/shard_map/ppermute | solution.py:66
  183.1 7.4 %copy-start.1 = (bf16[1,1024,320]{2,1,0:T(8,128)(2,1)S(1)}, bf16[1,1024,320]{2,1,0:T(8,128)(2,1)}, u32[]{:S(2)}) copy-start(bf16[1,1024,320]{2,1,0:T(8,128)(2,1)} %all-gather) | copy-start | bytes 1966084
  183.1 7.4 %collective-permute-start.2 = (bf16[512,864]{0,1:T(8,128)(2,1)}, bf16[512,864]{0,1:T(8,128)(2,1)S(1)}, u32[]{:S(2)}, u32[]{:S(2)}) collective-permute-start(bf16[512,864]{0,1:T(8,128)(2,1)} %copy.14), channel_id=1, source_target_pairs={{0,1},{1,0},{2,3},{3,2},{4,5},{5,4},{6,7},{7,6},{8,9},{9,8},{10,11... | collective-permute-start | bytes 2654216 | tf_op jit(solution)/shard_map/ppermute | solution.py:74
Sparse Core Ops, SparseCore 0:
  16.5 90.7 all-gather.2

commit v2 on v1

v2 whole, which is shorter than its diff:
```python
import jax
import jax.numpy as jnp
from jax import lax
from jax.sharding import Mesh
from jax.sharding import PartitionSpec as P

SEQ_LEN = 512
SEQS = 2
NZ, NXH, NXL, NY, NCORE = 16, 2, 2, 4, 2
ROW = ("z", "xh")
COL = ("xl", "y", "core")
SWAP = [(0, 1), (1, 0)]
BF, F32 = jnp.bfloat16, jnp.float32
SPLIT = 896

def dot(a, b):
    return jnp.dot(a, b, preferred_element_type=F32)


def dot_t(a, b):
    return lax.dot_general(a, b, (((0,), (0,)), ((), ())), preferred_element_type=F32)


def total(x):
    out = x[0].astype(F32)
    for i in range(1, x.shape[0]):
        out = out + x[i].astype(F32)
    return out


def tie(*values):
    return lax.optimization_barrier(values)


def spread(x, axes, n):
    return lax.all_to_all(jnp.broadcast_to(x[None], (n,) + x.shape), axes, 0, 0)


def local(activations, act_basis, gradients, grad_basis):
    core = lax.axis_index("core")
    xh = lax.axis_index("xh")
    tokens, width = activations.shape
    cols = grad_basis.shape[1]
    n = NXL * NY

    def swap(x):
        return lax.ppermute(x, "xh", SWAP)

    def in_order(mine, other):
        return jnp.where(xh == 0, mine, other), jnp.where(xh == 0, other, mine)

    hidden, block = gradients.shape[1], act_basis.shape[0]
    pieces = [act_basis[i : i + tokens] for i in range(0, block, tokens)]
    count, act_cols = len(pieces), act_basis.shape[1]
    shared = lax.all_gather(jnp.concatenate([gradients] + pieces, axis=1), "z", axis=0, tiled=True)

    parts = activations.reshape(tokens, NZ, NXH, count, tokens).transpose(2, 3, 0, 1, 4)
    parts = parts.reshape(NXH, count, tokens, NZ * tokens)
    mine, other = in_order(parts[0], parts[1])
    parts = jnp.concatenate([mine, swap(other)], axis=1)
    grad_basis, parts = tie(grad_basis, parts)
    basis_other = swap(grad_basis)

    acts = sum(
        dot(parts[i], shared[:, hidden + i * act_cols : hidden + (i + 1) * act_cols])
        for i in range(count)
    )
    acts_swapped = swap(acts[tokens:])

    half = tokens * NZ // SEQS

    def partial(seq):
        rows = [
            lax.dynamic_slice(shared, (seq * half, lo), (half, hi - lo))
            for lo, hi in ((0, SPLIT), (SPLIT, hidden))
        ]
        return [
            dot(rows[0], b[:SPLIT]) + dot(rows[1], b[SPLIT:]) for b in (grad_basis, basis_other)
        ]

    sums = [
        (a + lax.ppermute(b, "core", SWAP)).astype(BF)
        for a, b in zip(partial(core), partial(1 - core))
    ]
    sums = jnp.stack(in_order(*sums)).reshape(NXH * n, half // n, cols)
    acts, acts_swapped, sums = tie(acts, acts_swapped, sums)
    sums = lax.all_to_all(sums, ("xh", "xl", "y"), 0, 0)
    acts = (acts[:tokens] + acts_swapped).astype(BF)
    acts = lax.all_gather(acts, "z")
    acts, sums = tie(acts, sums)
    acts = jnp.stack(in_order(acts, swap(acts)), axis=1).reshape(SEQS * SEQ_LEN, act_cols)

    sums = sums.reshape(NXH, n, half // n, cols)
    own = jnp.stack([total(sums[h]).astype(BF) for h in range(NXH)])
    own = spread(own, ("xl", "y"), n).reshape(SEQ_LEN, cols)
    rest = lax.ppermute(own, "core", SWAP)

    def seq_grad(seq, g):
        return dot_t(lax.dynamic_slice_in_dim(acts, seq * SEQ_LEN, SEQ_LEN, 0), g)

    first, second = seq_grad(core, own), seq_grad(1 - core, rest)
    return (first * first + second * second) / (SEQS * SEQ_LEN)


def solution(mesh):
    split = Mesh(
        mesh.devices.reshape(NZ, NXH, NXL, NY, NCORE), ("z", "xh", "xl", "y", "core")
    )
    return jax.shard_map(
        local,
        mesh=split,
        in_specs=(P(ROW, None), P(ROW, COL), P(ROW, COL), P(COL, ROW)),
        out_specs=P(COL, ROW),
        check_vma=False,
    )
```

time: 200 us -> 185 us (0.925)
  blocking collectives: 107 us -> 25.1 us
  waiting for transfers between devices: 14.5 us -> 65.1 us
  starting transfers between devices: 36.3 us -> 54.2 us
  local copies, waits for them, and re-layouts: 11.9 us -> 9.1 us
    all_gather x1, waiting for transfers between devices: 0.01 us -> 57.5 us  [local(): lax.all_gather(jnp.concatenate([gradients] + pieces, axis=1), 'z', axis=0...]
    all_gather x2 -> x1, blocking collectives: 73.2 us -> 25.1 us  [local(): acts = lax.all_gather(acts, 'z')]
    all_to_all x2 -> x0, blocking collectives: 33.4 us -> none  [the longest x1 18.2 us: local(): lax.all_to_all(partial.reshape(n, SEQ_LEN // n, cols), ('xl', 'y'), 0, 0)]
    ppermute x2 -> x6, starting transfers between devices: 18.8 us -> 33.2 us  [the longest x4 19.8 us: swap(): return lax.ppermute(x, 'xh', SWAP)]
    ppermute x1, starting transfers between devices: 5.15 us -> 11.7 us  [local(): rest = lax.ppermute(own, 'core', SWAP)]
    ppermute x2 -> x6, waiting for transfers between devices: 6 us -> 2 us  [the longest x4 1.99 us: swap(): return lax.ppermute(x, 'xh', SWAP)]
    reshape x3 -> x2, local copies, waits for them, and re-layouts: 6.85 us -> 2.89 us  [the longest x1 2.38 us: local(): activations.reshape(tokens, NZ, NXH, count, tokens).transpose(2, 3, 0, 1, 4)]
    all_to_all x2, waiting for transfers between devices: 8.05 us -> 4.34 us  [the longest x1 4.33 us: spread(): return lax.all_to_all(jnp.broadcast_to(x[None], (n,) + x.shape), axes, 0, 0)]
  transfers between devices with their start and end apart: 6 -> 10, of which waited for: 4 -> 4; matrix products, arithmetic and copies ran while one was open for 5% -> 11% of each run, Pallas kernels for 0% -> 0%
where the time goes in v2:
time: 185 us; the launch traced here: 184 us
  waiting for transfers between devices  65.1 us (35%)
  starting transfers between devices  54.2 us (29%)
  blocking collectives  25.1 us (14%)
  matrix products  16 us (9%)
  between operations  13.7 us (7%)
  local copies, waits for them, and re-layouts  9.1 us (5%)
    all_gather x1, waiting for transfers between devices, local(): lax.all_gather(jnp.concatenate([gradients] + pieces, axis=1), 'z', axis=0...  57.5 us
    all_gather x1, blocking collectives, local(): acts = lax.all_gather(acts, 'z')  25.1 us
    ppermute x4, starting transfers between devices, swap(): return lax.ppermute(x, 'xh', SWAP)  19.8 us
    dot_general x13, matrix products, dot(): return jnp.dot(a, b, preferred_element_type=F32)  13.9 us
    ppermute x2, starting transfers between devices, local(): lax.ppermute(b, 'core', SWAP)  13.4 us
    ppermute x1, starting transfers between devices, local(): rest = lax.ppermute(own, 'core', SWAP)  11.7 us
    all_to_all x1, starting transfers between devices, local(): sums = lax.all_to_all(sums, ('xh', 'xl', 'y'), 0, 0)  4.72 us
    all_to_all x1, starting transfers between devices, spread(): return lax.all_to_all(jnp.broadcast_to(x[None], (n,) + x.shape), axes, 0, 0)  4.65 us
  transfers between devices with their start and end apart: 10, of which 4 were waited for; matrix products, arithmetic and copies ran while one was open for 11% of the time, Pallas kernels for 0%

profile of v2, /device:TPU:1, one launch (start us, length us, event | category | flops | bytes accessed | tf_op | source)
XLA Modules:
  0.0 184.0 jit_solution(12226805780211439427)
XLA Ops:
  7.4 1.7 concatenate.7
  9.1 2.4 %reshape.31 = bf16[32,16,2,5,32]{4,3,2,1,0:T(8,128)(2,1)S(1)} reshape(bf16[32,5120]{1,0:T(8,128)(2,1)} %param.4) | data formatting | bytes 655360 | tf_op jit(solution)/shard_map/reshape | solution.py:57
  12.4 5.5 %collective-permute-start = (bf16[5,32,512]{2,1,0:T(8,128)(2,1)S(1)}, bf16[5,32,512]{2,1,0:T(8,128)(2,1)S(1)}, u32[]{:S(2)}, u32[]{:S(2)}) collective-permute-start(bf16[5,32,512]{2,1,0:T(8,128)(2,1)S(1)} %select_n.61), channel_id=1, source_target_pairs={{0,16},{16,0},{1,17},{17,1},{2,18},{18,2},{3,19},{19,3},{4,20},{20... | collective-permute-start | bytes 491528 | tf_op jit(solution)/shard_map/ppermute | solution.py:47
  18.6 2.0 %collective-permute-done = bf16[5,32,512]{2,1,0:T(8,128)(2,1)S(1)} collective-permute-done((bf16[5,32,512]{2,1,0:T(8,128)(2,1)S(1)}, bf16[5,32,512]{2,1,0:T(8,128)(2,1)S(1)}, u32[]{:S(2)}, u32[]{:S(2)}) %collective-permute-start) | collective-permute-done | bytes 163872 | tf_op jit(solution)/shard_map/ppermute | solution.py:47
  20.6 4.9 %collective-permute-start.3 = (bf16[1728,864]{1,0:T(8,128)(2,1)}, bf16[1728,864]{1,0:T(8,128)(2,1)S(1)}, u32[]{:S(2)}, u32[]{:S(2)}) collective-permute-start(bf16[1728,864]{1,0:T(8,128)(2,1)} %param.7), channel_id=1, source_target_pairs={{0,16},{16,0},{1,17},{17,1},{2,18},{18,2},{3,19},{19,3},{4,20},{20... | collective-permute-start | bytes 8957960 | tf_op jit(solution)/shard_map/ppermute | solution.py:47
  25.5 57.5 %all-gather.3.cloned.1.call-done = bf16[512,3328]{1,0:T(8,128)(2,1)} async-done(((bf16[32,3328]{1,0:T(8,128)(2,1)}), bf16[512,3328]{1,0:T(8,128)(2,1)}) %all-gather.3.cloned.1.call-update) | async-done | bytes 3407888 | tf_op jit(solution)/shard_map/all_gather | solution.py:55
  83.0 1.5 fusion.54
  84.5 1.2 convolution_add_fusion.3
  85.7 1.4 convolution_add_fusion.2
  87.1 1.2 convolution_add_fusion.1
  88.3 1.3 convolution_add_fusion
  89.6 4.9 %collective-permute-start.1 = (f32[32,320]{1,0:T(8,128)S(1)}, f32[32,320]{1,0:T(8,128)S(1)}, u32[]{:S(2)}, u32[]{:S(2)}) collective-permute-start(f32[32,320]{1,0:T(8,128)S(1)} %slice.191), channel_id=1, source_target_pairs={{0,16},{16,0},{1,17},{17,1},{2,18},{18,2},{3,19},{19,3},{4,20},{20... | collective-permute-start | bytes 122888 | tf_op jit(solution)/shard_map/ppermute | solution.py:47
  94.6 1.8 fusion.28
  97.2 11.5 %collective-permute-start.4 = (f32[256,864]{0,1:T(8,128)S(1)}, f32[256,864]{0,1:T(8,128)S(1)}, u32[]{:S(2)}, u32[]{:S(2)}) collective-permute-start(f32[256,864]{0,1:T(8,128)S(1)} %fusion.25), channel_id=1, source_target_pairs={{0,1},{1,0},{2,3},{3,2},{4,5},{5,4},{6,7},{7,6},{8,9},{9,8},{10,11... | collective-permute-start | bytes 2654216 | tf_op jit(solution)/shard_map/ppermute | solution.py:82
  110.3 1.9 %collective-permute-start.2 = (f32[256,864]{0,1:T(8,128)S(1)}, f32[256,864]{0,1:T(8,128)S(1)}, u32[]{:S(2)}, u32[]{:S(2)}) collective-permute-start(f32[256,864]{0,1:T(8,128)S(1)} %fusion.16), channel_id=1, source_target_pairs={{0,1},{1,0},{2,3},{3,2},{4,5},{5,4},{6,7},{7,6},{8,9},{9,8},{10,11... | collective-permute-start | bytes 2654216 | tf_op jit(solution)/shard_map/ppermute | solution.py:82
  115.5 1.3 copy.16
  116.8 4.7 %all-to-all-start = ((bf16[16,32,864]{2,1,0:T(8,128)(2,1)}), bf16[16,32,864]{2,1,0:T(8,128)(2,1)S(1)}, u32[]{:S(2)}, u32[]{:S(2)}) async-start(bf16[16,32,864]{2,1,0:T(8,128)(2,1)} %bitcast.8), calls=%async_computation | async-start | bytes 1835008 | tf_op jit(solution)/shard_map/all_to_all | solution.py:87
  121.6 25.1 %all-gather = bf16[512,320]{1,0:T(8,128)(2,1)S(1)} all-gather(bf16[32,320]{1,0:T(8,128)(2,1)S(1)} %add_convert_fusion.2), channel_id=2, replica_groups=mesh['z'=16,'xh'=2,'xl'=2,'y'=4,'core'=2] {'z'}, dimensions={0}, use_global_device_ids=true | all-gather | bytes 348160 | tf_op jit(solution)/shard_map/all_gather | solution.py:89
  147.8 4.6 %all-to-all-start.1 = ((bf16[8,2,32,864]{3,2,1,0:T(8,128)(2,1)}), bf16[8,2,32,864]{3,2,1,0:T(8,128)(2,1)S(1)}, u32[]{:S(2)}, u32[]{:S(2)}) async-start(bf16[8,2,32,864]{3,2,1,0:T(8,128)(2,1)} %broadcast_in_dim.2), calls=%async_computation.1 | async-start | bytes 1835008 | tf_op jit(solution)/shard_map/all_to_all | solution.py:36
  152.5 4.5 %collective-permute-start.5 = (bf16[16,32,320]{2,1,0:T(8,128)(2,1)S(1)}, bf16[16,32,320]{2,1,0:T(8,128)(2,1)S(1)}, u32[]{:S(2)}, u32[]{:S(2)}) collective-permute-start(bf16[16,32,320]{2,1,0:T(8,128)(2,1)S(1)} %bitcast.41), channel_id=1, source_target_pairs={{0,16},{16,0},{1,17},{17,1},{2,18},{18,2},{3,19},{19,3},{4,20},{20... | collective-permute-start | bytes 983048 | tf_op jit(solution)/shard_map/ppermute | solution.py:47
  157.0 4.3 %all-to-all-done.1 = bf16[8,2,32,864]{3,2,1,0:T(8,128)(2,1)S(1)} async-done(((bf16[8,2,32,864]{3,2,1,0:T(8,128)(2,1)}), bf16[8,2,32,864]{3,2,1,0:T(8,128)(2,1)S(1)}, u32[]{:S(2)}, u32[]{:S(2)}) %all-to-all-start.1) | async-done | bytes 884768 | tf_op jit(solution)/shard_map/all_to_all | solution.py:36
  161.8 11.7 %collective-permute-start.6 = (bf16[512,864]{0,1:T(8,128)(2,1)S(1)}, bf16[512,864]{0,1:T(8,128)(2,1)S(1)}, u32[]{:S(2)}, u32[]{:S(2)}) collective-permute-start(bf16[512,864]{0,1:T(8,128)(2,1)S(1)} %copy.18), channel_id=1, source_target_pairs={{0,1},{1,0},{2,3},{3,2},{4,5},{5,4},{6,7},{7,6},{8,9},{9,8},{10,11... | collective-permute-start | bytes 2654216 | tf_op jit(solution)/shard_map/ppermute | solution.py:96
  174.3 1.2 collective-permute-done.6
  175.5 1.6 fusion.9
  (36 shorter events, 10.5 us)
Async XLA Ops:
  6.5 76.5 %all-gather.3.cloned.1.call-start = ((), (), s32[]{:S(2)}) async-start(), calls=%async_computation.2 | async-start | bytes 3620864 | tf_op jit(solution)/shard_map/all_gather | solution.py:55
  12.4 8.2 %collective-permute-start = (bf16[5,32,512]{2,1,0:T(8,128)(2,1)S(1)}, bf16[5,32,512]{2,1,0:T(8,128)(2,1)S(1)}, u32[]{:S(2)}, u32[]{:S(2)}) collective-permute-start(bf16[5,32,512]{2,1,0:T(8,128)(2,1)S(1)} %select_n.61), channel_id=1, source_target_pairs={{0,16},{16,0},{1,17},{17,1},{2,18},{18,2},{3,19},{19,3},{4,20},{20... | collective-permute-start | bytes 491528 | tf_op jit(solution)/shard_map/ppermute | solution.py:47
  20.6 73.9 %collective-permute-start.3 = (bf16[1728,864]{1,0:T(8,128)(2,1)}, bf16[1728,864]{1,0:T(8,128)(2,1)S(1)}, u32[]{:S(2)}, u32[]{:S(2)}) collective-permute-start(bf16[1728,864]{1,0:T(8,128)(2,1)} %param.7), channel_id=1, source_target_pairs={{0,16},{16,0},{1,17},{17,1},{2,18},{18,2},{3,19},{19,3},{4,20},{20... | collective-permute-start | bytes 8957960 | tf_op jit(solution)/shard_map/ppermute | solution.py:47
  83.0 13.3 %copy-start = (bf16[512,3328]{1,0:T(8,128)(2,1)S(1)}, bf16[512,3328]{1,0:T(8,128)(2,1)}, u32[]{:S(2)}) copy-start(bf16[512,3328]{1,0:T(8,128)(2,1)} %all-gather.3.cloned.1.call-done) | copy-start | bytes 10223620
  89.6 19.1 %copy-start.1 = (bf16[1728,864]{1,0:T(8,128)(2,1)S(1)}, bf16[1728,864]{1,0:T(8,128)(2,1)}, u32[]{:S(2)}) copy-start(bf16[1728,864]{1,0:T(8,128)(2,1)} %param.7) | copy-start | bytes 8957956
  89.6 27.2 %collective-permute-start.1 = (f32[32,320]{1,0:T(8,128)S(1)}, f32[32,320]{1,0:T(8,128)S(1)}, u32[]{:S(2)}, u32[]{:S(2)}) collective-permute-start(f32[32,320]{1,0:T(8,128)S(1)} %slice.191), channel_id=1, source_target_pairs={{0,16},{16,0},{1,17},{17,1},{2,18},{18,2},{3,19},{19,3},{4,20},{20... | collective-permute-start | bytes 122888 | tf_op jit(solution)/shard_map/ppermute | solution.py:47
  97.2 16.6 %collective-permute-start.4 = (f32[256,864]{0,1:T(8,128)S(1)}, f32[256,864]{0,1:T(8,128)S(1)}, u32[]{:S(2)}, u32[]{:S(2)}) collective-permute-start(f32[256,864]{0,1:T(8,128)S(1)} %fusion.25), channel_id=1, source_target_pairs={{0,1},{1,0},{2,3},{3,2},{4,5},{5,4},{6,7},{7,6},{8,9},{9,8},{10,11... | collective-permute-start | bytes 2654216 | tf_op jit(solution)/shard_map/ppermute | solution.py:82
  110.3 4.3 %collective-permute-start.2 = (f32[256,864]{0,1:T(8,128)S(1)}, f32[256,864]{0,1:T(8,128)S(1)}, u32[]{:S(2)}, u32[]{:S(2)}) collective-permute-start(f32[256,864]{0,1:T(8,128)S(1)} %fusion.16), channel_id=1, source_target_pairs={{0,1},{1,0},{2,3},{3,2},{4,5},{5,4},{6,7},{7,6},{8,9},{9,8},{10,11... | collective-permute-start | bytes 2654216 | tf_op jit(solution)/shard_map/ppermute | solution.py:82
  116.8 29.8 %all-to-all-start = ((bf16[16,32,864]{2,1,0:T(8,128)(2,1)}), bf16[16,32,864]{2,1,0:T(8,128)(2,1)S(1)}, u32[]{:S(2)}, u32[]{:S(2)}) async-start(bf16[16,32,864]{2,1,0:T(8,128)(2,1)} %bitcast.8), calls=%async_computation | async-start | bytes 1835008 | tf_op jit(solution)/shard_map/all_to_all | solution.py:87
  147.8 13.5 %all-to-all-start.1 = ((bf16[8,2,32,864]{3,2,1,0:T(8,128)(2,1)}), bf16[8,2,32,864]{3,2,1,0:T(8,128)(2,1)S(1)}, u32[]{:S(2)}, u32[]{:S(2)}) async-start(bf16[8,2,32,864]{3,2,1,0:T(8,128)(2,1)} %broadcast_in_dim.2), calls=%async_computation.1 | async-start | bytes 1835008 | tf_op jit(solution)/shard_map/all_to_all | solution.py:36
  152.5 21.1 %collective-permute-start.5 = (bf16[16,32,320]{2,1,0:T(8,128)(2,1)S(1)}, bf16[16,32,320]{2,1,0:T(8,128)(2,1)S(1)}, u32[]{:S(2)}, u32[]{:S(2)}) collective-permute-start(bf16[16,32,320]{2,1,0:T(8,128)(2,1)S(1)} %bitcast.41), channel_id=1, source_target_pairs={{0,16},{16,0},{1,17},{17,1},{2,18},{18,2},{3,19},{19,3},{4,20},{20... | collective-permute-start | bytes 983048 | tf_op jit(solution)/shard_map/ppermute | solution.py:47
  161.8 13.7 %collective-permute-start.6 = (bf16[512,864]{0,1:T(8,128)(2,1)S(1)}, bf16[512,864]{0,1:T(8,128)(2,1)S(1)}, u32[]{:S(2)}, u32[]{:S(2)}) collective-permute-start(bf16[512,864]{0,1:T(8,128)(2,1)S(1)} %copy.18), channel_id=1, source_target_pairs={{0,1},{1,0},{2,3},{3,2},{4,5},{5,4},{6,7},{7,6},{8,9},{9,8},{10,11... | collective-permute-start | bytes 2654216 | tf_op jit(solution)/shard_map/ppermute | solution.py:96
Sparse Core Ops, SparseCore 0:
  9.4 73.5 all-gather.2

commit v3 on v2

v3 whole, which is shorter than its diff:
```python
import jax
import jax.numpy as jnp
from jax import lax
from jax.sharding import Mesh
from jax.sharding import PartitionSpec as P

SEQ_LEN = 512
SEQS = 2
NZ, NXH, NXL, NY, NCORE = 16, 2, 2, 4, 2
ROW = ("z", "xh")
COL = ("xl", "y", "core")
SWAP = [(0, 1), (1, 0)]
BF, F32 = jnp.bfloat16, jnp.float32
SPLIT = 1024

PARITY = [[p + 2 * k for k in range(NZ // 2)] for p in range(2)]
QUADS = [[(2 * k + i) * NXH + h for i in range(2) for h in range(NXH)] for k in range(NZ // 2)]

def dot(a, b):
    return jnp.dot(a, b, preferred_element_type=F32)


def dot_t(a, b):
    return lax.dot_general(a, b, (((0,), (0,)), ((), ())), preferred_element_type=F32)


def total(x):
    out = x[0].astype(F32)
    for i in range(1, x.shape[0]):
        out = out + x[i].astype(F32)
    return out


def tie(*values):
    return lax.optimization_barrier(values)


def spread(x, axes, n):
    return lax.all_to_all(jnp.broadcast_to(x[None], (n,) + x.shape), axes, 0, 0)


def local(activations, act_basis, gradients, grad_basis):
    core = lax.axis_index("core")
    xh = lax.axis_index("xh")
    tokens, width = activations.shape
    cols = grad_basis.shape[1]
    n = NXL * NY

    def swap(x):
        return lax.ppermute(x, "xh", SWAP)

    def in_order(mine, other):
        return jnp.where(xh == 0, mine, other), jnp.where(xh == 0, other, mine)

    grads = lax.all_gather(gradients, "z", axis=0, tiled=True)

    block, act_cols = act_basis.shape
    parts = activations.reshape(tokens, NZ // 2, 4, block).transpose(2, 0, 1, 3)
    parts = parts.reshape(4, tokens, width // 4)
    parts = lax.all_to_all(parts, ROW, 0, 0, axis_index_groups=QUADS)
    first, second = grad_basis[:SPLIT], grad_basis[SPLIT:]
    first_other = swap(first)
    rows = lax.all_gather(act_basis, "z", axis=0, tiled=True, axis_index_groups=PARITY)
    acts = dot(parts.reshape(4 * tokens, width // 4), rows).reshape(4, tokens, act_cols)
    acts, first_other = tie(acts, first_other)
    second, acts = tie(second, acts)
    acts = lax.all_to_all(acts, ROW, 0, 0, axis_index_groups=QUADS)
    second_other = swap(second)
    acts = total(acts).astype(BF)
    seq, acts = tie(core, acts)
    acts = spread(acts, "z", NZ)

    half, hidden = tokens * NZ // SEQS, gradients.shape[1]

    def part(seq, lo, hi, basis):
        return dot(lax.dynamic_slice(grads, (seq * half, lo), (half, hi - lo)), basis)

    def products(seq, first, second):
        theirs = part(1 - seq, 0, SPLIT, first) + part(1 - seq, SPLIT, hidden, second)
        theirs = lax.ppermute(theirs, "core", SWAP)
        return (part(seq, 0, SPLIT, first) + part(seq, SPLIT, hidden, second) + theirs).astype(BF)

    sums = products(seq, first, second)
    second_other, sums, acts = tie(second_other, sums, acts)
    sums = in_order(sums, products(seq, first_other, second_other))
    sums = jnp.stack(sums).reshape(NXH * n, half // n, cols)
    sums = lax.all_to_all(sums, ("xh", "xl", "y"), 0, 0)
    acts = jnp.stack(in_order(acts, swap(acts)), axis=1).reshape(SEQS * SEQ_LEN, act_cols)

    sums = sums.reshape(NXH, n, half // n, cols)
    own = jnp.stack([total(sums[h]).astype(BF) for h in range(NXH)])
    own = spread(own, ("xl", "y"), n).reshape(SEQ_LEN, cols)
    rest = lax.ppermute(own, "core", SWAP)

    def seq_grad(seq, g):
        return dot_t(lax.dynamic_slice_in_dim(acts, seq * SEQ_LEN, SEQ_LEN, 0), g)

    first, second = seq_grad(core, own), seq_grad(1 - core, rest)
    return (first * first + second * second) / (SEQS * SEQ_LEN)


def solution(mesh):
    split = Mesh(
        mesh.devices.reshape(NZ, NXH, NXL, NY, NCORE), ("z", "xh", "xl", "y", "core")
    )
    return jax.shard_map(
        local,
        mesh=split,
        in_specs=(P(ROW, None), P(ROW, COL), P(ROW, COL), P(COL, ROW)),
        out_specs=P(COL, ROW),
        check_vma=False,
    )
```

time: 185 us -> 179 us (0.968)
  waiting for transfers between devices: 65.1 us -> 9.43 us
  blocking collectives: 25.1 us -> 57.5 us
  starting transfers between devices: 54.2 us -> 61.6 us
  matrix products: 16 us -> 22.5 us
    all_gather x1, waiting for transfers between devices: 57.5 us -> 0.02 us  [local(): grads = lax.all_gather(gradients, 'z', axis=0, tiled=True)]
    all_to_all x0 -> x1, blocking collectives: none -> 17.8 us  [local(): sums = lax.all_to_all(sums, ('xh', 'xl', 'y'), 0, 0)]
    all_gather x1, blocking collectives: 25.1 us -> 39.7 us  [local(): lax.all_gather(act_basis, 'z', axis=0, tiled=True, axis_index_groups=PARITY)]
    all_to_all x1 -> x2, starting transfers between devices: 4.65 us -> 11.9 us  [spread(): return lax.all_to_all(jnp.broadcast_to(x[None], (n,) + x.shape), axes, 0, 0)]
    dot_general x13 -> x9, matrix products: 13.9 us -> 20.3 us  [dot(): return jnp.dot(a, b, preferred_element_type=F32)]
    ppermute x4 -> x3, starting transfers between devices: 19.8 us -> 14 us  [swap(): return lax.ppermute(x, 'xh', SWAP)]
    all_to_all x1 -> x2, starting transfers between devices: 4.72 us -> 9.81 us  [the longest x1 6.22 us: local(): acts = lax.all_to_all(acts, ROW, 0, 0, axis_index_groups=QUADS)]
    ppermute x2, starting transfers between devices: 13.4 us -> 17.9 us  [products(): theirs = lax.ppermute(theirs, 'core', SWAP)]
  transfers between devices with their start and end apart: 10 -> 11, of which waited for: 4 -> 4; matrix products, arithmetic and copies ran while one was open for 11% -> 13% of each run, Pallas kernels for 0% -> 0%
where the time goes in v3:
time: 179 us; the launch traced here: 176 us
  starting transfers between devices  61.6 us (34%)
  blocking collectives  57.5 us (32%)
  matrix products  22.5 us (13%)
  between operations  13.7 us (8%)
  local copies, waits for them, and re-layouts  10.2 us (6%)
  waiting for transfers between devices  9.43 us (5%)
    all_gather x1, blocking collectives, local(): lax.all_gather(act_basis, 'z', axis=0, tiled=True, axis_index_groups=PARITY)  39.7 us
    dot_general x9, matrix products, dot(): return jnp.dot(a, b, preferred_element_type=F32)  20.3 us
    ppermute x2, starting transfers between devices, products(): theirs = lax.ppermute(theirs, 'core', SWAP)  17.9 us
    all_to_all x1, blocking collectives, local(): sums = lax.all_to_all(sums, ('xh', 'xl', 'y'), 0, 0)  17.8 us
    ppermute x3, starting transfers between devices, swap(): return lax.ppermute(x, 'xh', SWAP)  14 us
    all_to_all x2, starting transfers between devices, spread(): return lax.all_to_all(jnp.broadcast_to(x[None], (n,) + x.shape), axes, 0, 0)  11.9 us
    ppermute x1, starting transfers between devices, local(): rest = lax.ppermute(own, 'core', SWAP)  7.84 us
    all_to_all x2, waiting for transfers between devices, spread(): return lax.all_to_all(jnp.broadcast_to(x[None], (n,) + x.shape), axes, 0, 0)  6.28 us
  transfers between devices with their start and end apart: 11, of which 4 were waited for; matrix products, arithmetic and copies ran while one was open for 13% of the time, Pallas kernels for 0%

profile of v3, /device:TPU:1, one launch (start us, length us, event | category | flops | bytes accessed | tf_op | source)
XLA Modules:
  0.0 176.3 jit_solution(13183268568780597261)
XLA Ops:
  8.8 2.5 %copy.19 = bf16[1024,864]{0,1:T(8,128)(2,1)} copy(bf16[1024,864]{1,0:T(8,128)(2,1)S(1)} %slice-done) | data formatting | bytes 3538944
  11.2 5.5 %collective-permute-start = (bf16[1024,864]{0,1:T(8,128)(2,1)}, bf16[1024,864]{0,1:T(8,128)(2,1)S(1)}, u32[]{:S(2)}, u32[]{:S(2)}) collective-permute-start(bf16[1024,864]{0,1:T(8,128)(2,1)} %copy.19), channel_id=1, source_target_pairs={{0,16},{16,0},{1,17},{17,1},{2,18},{18,2},{3,19},{19,3},{4,20},{20... | collective-permute-start | bytes 5308424 | tf_op jit(solution)/shard_map/ppermute | solution.py:50
  18.7 3.6 %all-to-all-start = ((bf16[4,32,1280]{2,1,0:T(8,128)(2,1)}), bf16[4,32,1280]{2,1,0:T(8,128)(2,1)S(1)}, u32[]{:S(2)}, u32[]{:S(2)}) async-start(bf16[4,32,1280]{2,1,0:T(8,128)(2,1)} %reshape.35), calls=%async_computation | async-start | bytes 655360 | tf_op jit(solution)/shard_map/all_to_all | solution.py:60
  23.7 39.7 %all_gather.6 = bf16[1280,320]{1,0:T(8,128)(2,1)} all-gather(bf16[160,320]{1,0:T(8,128)(2,1)S(1)} %copy-done.1), channel_id=1, replica_groups={{0,64,128,192,256,320,384,448},{32,96,160,224,288,352,416,480},{1,65,12..., dimensions={0}, use_global_device_ids=true | all-gather | bytes 921600 | tf_op jit(solution)/shard_map/all_gather | solution.py:63
  63.3 2.2 %fusion.6 = f32[4,32,320]{2,1,0:T(8,128)} fusion(bf16[4,32,1280]{2,1,0:T(8,128)(2,1)S(1)} %all-to-all-done, bf16[1280,320]{1,0:T(8,128)(2,1)} %all_gather.6), kind=kOutput, calls=%fused_computation.12 | convolution fusion | flops 104857600 | bytes 1310720 | tf_op jit(solution)/shard_map/dot_general | solution.py:20
  65.5 6.2 %all-to-all-start.1 = ((f32[4,32,320]{2,1,0:T(8,128)}), f32[4,32,320]{2,1,0:T(8,128)S(1)}, u32[]{:S(2)}, u32[]{:S(2)}) async-start(f32[4,32,320]{2,1,0:T(8,128)} %fusion.6), calls=%async_computation.1 | async-start | bytes 393216 | tf_op jit(solution)/shard_map/all_to_all | solution.py:67
  71.8 4.9 %collective-permute-start.1 = (bf16[704,864]{1,0:T(8,128)(2,1)S(1)}, bf16[704,864]{1,0:T(8,128)(2,1)}, u32[]{:S(2)}, u32[]{:S(2)}) collective-permute-start(bf16[704,864]{1,0:T(8,128)(2,1)S(1)} %slice.88), channel_id=1, source_target_pairs={{0,16},{16,0},{1,17},{17,1},{2,18},{18,2},{3,19},{19,3},{4,20},{20... | collective-permute-start | bytes 3649544 | tf_op jit(solution)/shard_map/ppermute | solution.py:50
  78.4 8.4 %all-to-all-start.2 = ((bf16[16,32,320]{2,1,0:T(8,128)(2,1)}), bf16[16,32,320]{2,1,0:T(8,128)(2,1)}, u32[]{:S(2)}, u32[]{:S(2)}) async-start(bf16[16,32,320]{2,1,0:T(8,128)(2,1)} %broadcast_in_dim.4), calls=%async_computation.2 | async-start | bytes 786432 | tf_op jit(solution)/shard_map/all_to_all | solution.py:39
  86.9 2.5 %fusion.9 = f32[256,864]{0,1:T(8,128)S(1)} fusion(bf16[512,1728]{1,0:T(8,128)(2,1)} %all-gather.2.cloned.1.call-done, s32[]{:T(128)S(6)} %select_n.44, bf16[1728,864]{1,0:T(8,128)(2,1)} %param.7), kind=kOutput, calls=%fused_computation.18 | convolution fusion | flops 452984832 | bytes 3244036 | tf_op jit(solution)/shard_map/dot_general | solution.py:20
  89.4 2.6 %convolution_add_fusion = f32[256,864]{0,1:T(8,128)} fusion(f32[256,864]{0,1:T(8,128)S(1)} %fusion.9, bf16[704,864]{1,0:T(8,128)(2,1)S(1)} %slice.88, bf16[512,1728]{1,0:T(8,128)(2,1)} %all-gather.2.cloned.1.call-done, s32[]{:T(128)S(6)} %select_n.44), kind=kOutput, calls=%fused_computation.4 | convolution fusion | flops 311648256 | bytes 3379204 | tf_op jit(solution)/shard_map/dot_general | solution.py:20
  92.0 9.1 %collective-permute-start.2 = (f32[256,864]{0,1:T(8,128)}, f32[256,864]{0,1:T(8,128)}, u32[]{:S(2)}, u32[]{:S(2)}) collective-permute-start(f32[256,864]{0,1:T(8,128)} %convolution_add_fusion), channel_id=1, source_target_pairs={{0,1},{1,0},{2,3},{3,2},{4,5},{5,4},{6,7},{7,6},{8,9},{9,8},{10,11... | collective-permute-start | bytes 2654216 | tf_op jit(solution)/shard_map/ppermute | solution.py:80
  101.0 2.5 %fusion.12 = f32[256,864]{0,1:T(8,128)S(1)} fusion(bf16[512,1728]{1,0:T(8,128)(2,1)} %all-gather.2.cloned.1.call-done, s32[]{:T(128)S(6)} %select_n.43, bf16[1728,864]{1,0:T(8,128)(2,1)} %param.7), kind=kOutput, calls=%fused_computation.21 | convolution fusion | flops 452984832 | bytes 3244036 | tf_op jit(solution)/shard_map/dot_general | solution.py:20
  103.6 2.0 %fusion.4 = bf16[256,864]{0,1:T(8,128)(2,1)S(1)} fusion(f32[256,864]{0,1:T(8,128)} %collective-permute-done.2, f32[256,864]{0,1:T(8,128)S(1)} %fusion.12, bf16[704,864]{1,0:T(8,128)(2,1)S(1)} %slice.88, bf16[512,1728]{1,0:T(8,128)(2,1)} %all-gather.2.cloned.1.call-done, s32[]{:T(128)S(6)} %select_n.43), kind=kOutput, calls=%fused_computation.10 | convolution fusion | flops 312090624 | bytes 3821572 | tf_op jit(solution)/shard_map/dot_general | solution.py:20
  105.6 2.1 %fusion.16 = f32[256,864]{0,1:T(8,128)S(1)} fusion(bf16[704,864]{1,0:T(8,128)(2,1)} %collective-permute-done.1, bf16[512,1728]{1,0:T(8,128)(2,1)} %all-gather.2.cloned.1.call-done, s32[]{:T(128)S(6)} %select_n.44), kind=kOutput, calls=%fused_computation.29 | convolution fusion | flops 311427072 | bytes 2539524 | tf_op jit(solution)/shard_map/dot_general | solution.py:20
  107.6 2.6 %convolution_add_fusion.2 = f32[256,864]{0,1:T(8,128)} fusion(f32[256,864]{0,1:T(8,128)S(1)} %fusion.16, bf16[1024,864]{0,1:T(8,128)(2,1)S(1)} %collective-permute-done, bf16[512,1728]{1,0:T(8,128)(2,1)} %all-gather.2.cloned.1.call-done, s32[]{:T(128)S(6)} %select_n.44), kind=kOutput, calls=%fused_computation.6 | convolution fusion | flops 453206016 | bytes 4063236 | tf_op jit(solution)/shard_map/dot_general | solution.py:20
  110.3 8.9 %collective-permute-start.4 = (f32[256,864]{0,1:T(8,128)}, f32[256,864]{0,1:T(8,128)S(1)}, u32[]{:S(2)}, u32[]{:S(2)}) collective-permute-start(f32[256,864]{0,1:T(8,128)} %convolution_add_fusion.2), channel_id=1, source_target_pairs={{0,1},{1,0},{2,3},{3,2},{4,5},{5,4},{6,7},{7,6},{8,9},{9,8},{10,11... | collective-permute-start | bytes 2654216 | tf_op jit(solution)/shard_map/ppermute | solution.py:80
  119.1 2.1 %fusion.19 = f32[256,864]{0,1:T(8,128)S(1)} fusion(bf16[704,864]{1,0:T(8,128)(2,1)} %collective-permute-done.1, bf16[512,1728]{1,0:T(8,128)(2,1)} %all-gather.2.cloned.1.call-done, s32[]{:T(128)S(6)} %select_n.43), kind=kOutput, calls=%fused_computation.32 | convolution fusion | flops 311427072 | bytes 2539524 | tf_op jit(solution)/shard_map/dot_general | solution.py:20
  121.4 1.8 fusion.5
  123.9 17.8 %all_to_all.25 = bf16[16,32,864]{2,1,0:T(8,128)(2,1)S(1)} all-to-all(bf16[16,32,864]{2,1,0:T(8,128)(2,1)S(1)} %bitcast.34), channel_id=1, replica_groups=mesh['z'=16,'xh'=2,'xl'=2,'y'=4,'core'=2] {'xh','xl','y'}, dimensions={0} | all-to-all | bytes 1769472 | tf_op jit(solution)/shard_map/all_to_all | solution.py:87
  142.9 3.6 %all-to-all-start.4 = ((bf16[8,2,32,864]{3,2,1,0:T(8,128)(2,1)}), bf16[8,2,32,864]{3,2,1,0:T(8,128)(2,1)S(1)}, u32[]{:S(2)}, u32[]{:S(2)}) async-start(bf16[8,2,32,864]{3,2,1,0:T(8,128)(2,1)} %broadcast_in_dim.5), calls=%async_computation.4 | async-start | bytes 1835008 | tf_op jit(solution)/shard_map/all_to_all | solution.py:39
  146.5 3.7 %collective-permute-start.3 = (bf16[16,32,320]{2,1,0:T(8,128)(2,1)}, bf16[16,32,320]{2,1,0:T(8,128)(2,1)S(1)}, u32[]{:S(2)}, u32[]{:S(2)}) collective-permute-start(bf16[16,32,320]{2,1,0:T(8,128)(2,1)} %all-to-all-done.2), channel_id=1, source_target_pairs={{0,16},{16,0},{1,17},{17,1},{2,18},{18,2},{3,19},{19,3},{4,20},{20... | collective-permute-start | bytes 983048 | tf_op jit(solution)/shard_map/ppermute | solution.py:50
  150.2 6.3 %all-to-all-done.4 = bf16[8,2,32,864]{3,2,1,0:T(8,128)(2,1)S(1)} async-done(((bf16[8,2,32,864]{3,2,1,0:T(8,128)(2,1)}), bf16[8,2,32,864]{3,2,1,0:T(8,128)(2,1)S(1)}, u32[]{:S(2)}, u32[]{:S(2)}) %all-to-all-start.4) | async-done | bytes 884768 | tf_op jit(solution)/shard_map/all_to_all | solution.py:39
  157.0 7.8 %collective-permute-start.5 = (bf16[512,864]{0,1:T(8,128)(2,1)S(1)}, bf16[512,864]{0,1:T(8,128)(2,1)S(1)}, u32[]{:S(2)}, u32[]{:S(2)}) collective-permute-start(bf16[512,864]{0,1:T(8,128)(2,1)S(1)} %copy.18), channel_id=1, source_target_pairs={{0,1},{1,0},{2,3},{3,2},{4,5},{5,4},{6,7},{7,6},{8,9},{9,8},{10,11... | collective-permute-start | bytes 2654216 | tf_op jit(solution)/shard_map/ppermute | solution.py:93
  167.9 1.6 fusion.1
  (34 shorter events, 12.9 us)
Async XLA Ops:
  6.5 80.3 %all-gather.2.cloned.1.call-start = ((), (), s32[]{:S(2)}) async-start(), calls=%async_computation.5 | async-start | bytes 1949696 | tf_op jit(solution)/shard_map/all_gather | solution.py:55
  7.3 1.5 slice-start
  8.8 8.0 %copy-start = (bf16[32,5120]{1,0:T(8,128)(2,1)S(1)}, bf16[32,5120]{1,0:T(8,128)(2,1)}, u32[]{:S(2)}) copy-start(bf16[32,5120]{1,0:T(8,128)(2,1)} %param.4) | copy-start | bytes 983044
  11.2 54.3 %collective-permute-start = (bf16[1024,864]{0,1:T(8,128)(2,1)}, bf16[1024,864]{0,1:T(8,128)(2,1)S(1)}, u32[]{:S(2)}, u32[]{:S(2)}) collective-permute-start(bf16[1024,864]{0,1:T(8,128)(2,1)} %copy.19), channel_id=1, source_target_pairs={{0,16},{16,0},{1,17},{17,1},{2,18},{18,2},{3,19},{19,3},{4,20},{20... | collective-permute-start | bytes 5308424 | tf_op jit(solution)/shard_map/ppermute | solution.py:50
  18.7 5.0 %copy-start.1 = (bf16[160,320]{1,0:T(8,128)(2,1)S(1)}, bf16[160,320]{1,0:T(8,128)(2,1)}, u32[]{:S(2)}) copy-start(bf16[160,320]{1,0:T(8,128)(2,1)} %param.5) | copy-start | bytes 307204
  18.7 44.7 %all-to-all-start = ((bf16[4,32,1280]{2,1,0:T(8,128)(2,1)}), bf16[4,32,1280]{2,1,0:T(8,128)(2,1)S(1)}, u32[]{:S(2)}, u32[]{:S(2)}) async-start(bf16[4,32,1280]{2,1,0:T(8,128)(2,1)} %reshape.35), calls=%async_computation | async-start | bytes 655360 | tf_op jit(solution)/shard_map/all_to_all | solution.py:60
  65.5 12.1 %all-to-all-start.1 = ((f32[4,32,320]{2,1,0:T(8,128)}), f32[4,32,320]{2,1,0:T(8,128)S(1)}, u32[]{:S(2)}, u32[]{:S(2)}) async-start(f32[4,32,320]{2,1,0:T(8,128)} %fusion.6), calls=%async_computation.1 | async-start | bytes 393216 | tf_op jit(solution)/shard_map/all_to_all | solution.py:67
  71.8 33.8 %collective-permute-start.1 = (bf16[704,864]{1,0:T(8,128)(2,1)S(1)}, bf16[704,864]{1,0:T(8,128)(2,1)}, u32[]{:S(2)}, u32[]{:S(2)}) collective-permute-start(bf16[704,864]{1,0:T(8,128)(2,1)S(1)} %slice.88), channel_id=1, source_target_pairs={{0,16},{16,0},{1,17},{17,1},{2,18},{18,2},{3,19},{19,3},{4,20},{20... | collective-permute-start | bytes 3649544 | tf_op jit(solution)/shard_map/ppermute | solution.py:50
  78.4 27.1 %all-to-all-start.2 = ((bf16[16,32,320]{2,1,0:T(8,128)(2,1)}), bf16[16,32,320]{2,1,0:T(8,128)(2,1)}, u32[]{:S(2)}, u32[]{:S(2)}) async-start(bf16[16,32,320]{2,1,0:T(8,128)(2,1)} %broadcast_in_dim.4), calls=%async_computation.2 | async-start | bytes 786432 | tf_op jit(solution)/shard_map/all_to_all | solution.py:39
  92.0 11.6 %collective-permute-start.2 = (f32[256,864]{0,1:T(8,128)}, f32[256,864]{0,1:T(8,128)}, u32[]{:S(2)}, u32[]{:S(2)}) collective-permute-start(f32[256,864]{0,1:T(8,128)} %convolution_add_fusion), channel_id=1, source_target_pairs={{0,1},{1,0},{2,3},{3,2},{4,5},{5,4},{6,7},{7,6},{8,9},{9,8},{10,11... | collective-permute-start | bytes 2654216 | tf_op jit(solution)/shard_map/ppermute | solution.py:80
  110.3 11.1 %collective-permute-start.4 = (f32[256,864]{0,1:T(8,128)}, f32[256,864]{0,1:T(8,128)S(1)}, u32[]{:S(2)}, u32[]{:S(2)}) collective-permute-start(f32[256,864]{0,1:T(8,128)} %convolution_add_fusion.2), channel_id=1, source_target_pairs={{0,1},{1,0},{2,3},{3,2},{4,5},{5,4},{6,7},{7,6},{8,9},{9,8},{10,11... | collective-permute-start | bytes 2654216 | tf_op jit(solution)/shard_map/ppermute | solution.py:80
  142.9 13.5 %all-to-all-start.4 = ((bf16[8,2,32,864]{3,2,1,0:T(8,128)(2,1)}), bf16[8,2,32,864]{3,2,1,0:T(8,128)(2,1)S(1)}, u32[]{:S(2)}, u32[]{:S(2)}) async-start(bf16[8,2,32,864]{3,2,1,0:T(8,128)(2,1)} %broadcast_in_dim.5), calls=%async_computation.4 | async-start | bytes 1835008 | tf_op jit(solution)/shard_map/all_to_all | solution.py:39
  146.5 19.6 %collective-permute-start.3 = (bf16[16,32,320]{2,1,0:T(8,128)(2,1)}, bf16[16,32,320]{2,1,0:T(8,128)(2,1)S(1)}, u32[]{:S(2)}, u32[]{:S(2)}) collective-permute-start(bf16[16,32,320]{2,1,0:T(8,128)(2,1)} %all-to-all-done.2), channel_id=1, source_target_pairs={{0,16},{16,0},{1,17},{17,1},{2,18},{18,2},{3,19},{19,3},{4,20},{20... | collective-permute-start | bytes 983048 | tf_op jit(solution)/shard_map/ppermute | solution.py:50
  157.0 10.9 %collective-permute-start.5 = (bf16[512,864]{0,1:T(8,128)(2,1)S(1)}, bf16[512,864]{0,1:T(8,128)(2,1)S(1)}, u32[]{:S(2)}, u32[]{:S(2)}) collective-permute-start(bf16[512,864]{0,1:T(8,128)(2,1)S(1)} %copy.18), channel_id=1, source_target_pairs={{0,1},{1,0},{2,3},{3,2},{4,5},{5,4},{6,7},{7,6},{8,9},{9,8},{10,11... | collective-permute-start | bytes 2654216 | tf_op jit(solution)/shard_map/ppermute | solution.py:93
Sparse Core Ops, SparseCore 0:
  9.4 75.6 all-gather.1

commit v4 on v3

--- a/solution.py
+++ b/solution.py
@@ -72,17 +72,21 @@
 
     half, hidden = tokens * NZ // SEQS, gradients.shape[1]
 
-    def part(seq, lo, hi, basis):
-        return dot(lax.dynamic_slice(grads, (seq * half, lo), (half, hi - lo)), basis)
+    def rows_of(seq):
+        return [
+            lax.dynamic_slice(grads, (seq * half, lo), (half, hi - lo))
+            for lo, hi in ((0, SPLIT), (SPLIT, hidden))
+        ]
 
-    def products(seq, first, second):
-        theirs = part(1 - seq, 0, SPLIT, first) + part(1 - seq, SPLIT, hidden, second)
-        theirs = lax.ppermute(theirs, "core", SWAP)
-        return (part(seq, 0, SPLIT, first) + part(seq, SPLIT, hidden, second) + theirs).astype(BF)
+    mine, theirs = tie(rows_of(seq), rows_of(1 - seq))
 
-    sums = products(seq, first, second)
+    def products(first, second):
+        added = lax.ppermute(dot(theirs[0], first) + dot(theirs[1], second), "core", SWAP)
+        return (dot(mine[0], first) + dot(mine[1], second) + added).astype(BF)
+
+    sums = products(first, second)
     second_other, sums, acts = tie(second_other, sums, acts)
-    sums = in_order(sums, products(seq, first_other, second_other))
+    sums = in_order(sums, products(first_other, second_other))
     sums = jnp.stack(sums).reshape(NXH * n, half // n, cols)
     sums = lax.all_to_all(sums, ("xh", "xl", "y"), 0, 0)
     acts = jnp.stack(in_order(acts, swap(acts)), axis=1).reshape(SEQS * SEQ_LEN, act_cols)

time: 179 us -> 176 us (0.983)
  matrix products: 22.5 us -> 14.6 us
  local copies, waits for them, and re-layouts: 10.2 us -> 13 us
    dot_general x9, matrix products: 20.3 us -> 12.4 us  [dot(): return jnp.dot(a, b, preferred_element_type=F32)]
    dynamic_slice x0 -> x2, local copies, waits for them, and re-layouts: none -> 2.75 us  [rows_of(): lax.dynamic_slice(grads, (seq * half, lo), (half, hi - lo))]
    unnamed x7 -> x21, local copies, waits for them, and re-layouts: 3.98 us -> 4.01 us
  transfers between devices with their start and end apart: 11 -> 11, of which waited for: 4 -> 5; matrix products, arithmetic and copies ran while one was open for 13% -> 11% of each run, Pallas kernels for 0% -> 0%
where the time goes in v4:
time: 176 us; the launch traced here: 174 us
  starting transfers between devices  62.4 us (35%)
  blocking collectives  58.7 us (33%)
  matrix products  14.6 us (8%)
  between operations  13.8 us (8%)
  local copies, waits for them, and re-layouts  13 us (7%)
  waiting for transfers between devices  10.6 us (6%)
    all_gather x1, blocking collectives, local(): lax.all_gather(act_basis, 'z', axis=0, tiled=True, axis_index_groups=PARITY)  39.6 us
    all_to_all x1, blocking collectives, local(): sums = lax.all_to_all(sums, ('xh', 'xl', 'y'), 0, 0)  19.1 us
    ppermute x2, starting transfers between devices, products(): lax.ppermute(dot(theirs[0], first) + dot(theirs[1], second), 'core', SWAP)  18.2 us
    ppermute x3, starting transfers between devices, swap(): return lax.ppermute(x, 'xh', SWAP)  14 us
    all_to_all x2, starting transfers between devices, spread(): return lax.all_to_all(jnp.broadcast_to(x[None], (n,) + x.shape), axes, 0, 0)  12.6 us
    dot_general x9, matrix products, dot(): return jnp.dot(a, b, preferred_element_type=F32)  12.4 us
    ppermute x1, starting transfers between devices, local(): rest = lax.ppermute(own, 'core', SWAP)  7.74 us
    all_to_all x1, starting transfers between devices, local(): acts = lax.all_to_all(acts, ROW, 0, 0, axis_index_groups=QUADS)  6.42 us
  transfers between devices with their start and end apart: 11, of which 5 were waited for; matrix products, arithmetic and copies ran while one was open for 11% of the time, Pallas kernels for 0%

profile of v4, /device:TPU:1, one launch (start us, length us, event | category | flops | bytes accessed | tf_op | source)
XLA Modules:
  0.0 174.5 jit_solution(15958517166686446061)
XLA Ops:
  7.3 1.5 slice-done
  8.8 2.4 %copy.19 = bf16[1024,864]{0,1:T(8,128)(2,1)} copy(bf16[1024,864]{1,0:T(8,128)(2,1)S(1)} %slice-done) | data formatting | bytes 3538944
  11.2 5.5 %collective-permute-start = (bf16[1024,864]{0,1:T(8,128)(2,1)}, bf16[1024,864]{0,1:T(8,128)(2,1)S(1)}, u32[]{:S(2)}, u32[]{:S(2)}) collective-permute-start(bf16[1024,864]{0,1:T(8,128)(2,1)} %copy.19), channel_id=1, source_target_pairs={{0,16},{16,0},{1,17},{17,1},{2,18},{18,2},{3,19},{19,3},{4,20},{20... | collective-permute-start | bytes 5308424 | tf_op jit(solution)/shard_map/ppermute | solution.py:50
  18.6 3.5 %all-to-all-start = ((bf16[4,32,1280]{2,1,0:T(8,128)(2,1)}), bf16[4,32,1280]{2,1,0:T(8,128)(2,1)S(1)}, u32[]{:S(2)}, u32[]{:S(2)}) async-start(bf16[4,32,1280]{2,1,0:T(8,128)(2,1)} %reshape.35), calls=%async_computation | async-start | bytes 655360 | tf_op jit(solution)/shard_map/all_to_all | solution.py:60
  22.1 1.4 slice.88
  23.5 39.6 %all_gather.6 = bf16[1280,320]{1,0:T(8,128)(2,1)} all-gather(bf16[160,320]{1,0:T(8,128)(2,1)S(1)} %copy-done.8), channel_id=1, replica_groups={{0,64,128,192,256,320,384,448},{32,96,160,224,288,352,416,480},{1,65,12..., dimensions={0}, use_global_device_ids=true | all-gather | bytes 921600 | tf_op jit(solution)/shard_map/all_gather | solution.py:63
  63.1 2.2 %fusion.6 = f32[4,32,320]{2,1,0:T(8,128)} fusion(bf16[4,32,1280]{2,1,0:T(8,128)(2,1)S(1)} %all-to-all-done, bf16[1280,320]{1,0:T(8,128)(2,1)} %all_gather.6), kind=kOutput, calls=%fused_computation.12 | convolution fusion | flops 104857600 | bytes 1310720 | tf_op jit(solution)/shard_map/dot_general | solution.py:20
  65.3 6.4 %all-to-all-start.1 = ((f32[4,32,320]{2,1,0:T(8,128)}), f32[4,32,320]{2,1,0:T(8,128)S(1)}, u32[]{:S(2)}, u32[]{:S(2)}) async-start(f32[4,32,320]{2,1,0:T(8,128)} %fusion.6), calls=%async_computation.1 | async-start | bytes 393216 | tf_op jit(solution)/shard_map/all_to_all | solution.py:67
  71.7 4.9 %collective-permute-start.1 = (bf16[704,864]{1,0:T(8,128)(2,1)S(1)}, bf16[704,864]{1,0:T(8,128)(2,1)}, u32[]{:S(2)}, u32[]{:S(2)}) collective-permute-start(bf16[704,864]{1,0:T(8,128)(2,1)S(1)} %slice.88), channel_id=1, source_target_pairs={{0,16},{16,0},{1,17},{17,1},{2,18},{18,2},{3,19},{19,3},{4,20},{20... | collective-permute-start | bytes 3649544 | tf_op jit(solution)/shard_map/ppermute | solution.py:50
  78.3 9.0 %all-to-all-start.2 = ((bf16[16,32,320]{2,1,0:T(8,128)(2,1)}), bf16[16,32,320]{2,1,0:T(8,128)(2,1)}, u32[]{:S(2)}, u32[]{:S(2)}) async-start(bf16[16,32,320]{2,1,0:T(8,128)(2,1)} %broadcast_in_dim.4), calls=%async_computation.2 | async-start | bytes 786432 | tf_op jit(solution)/shard_map/all_to_all | solution.py:39
  87.3 1.3 constant_dynamic-slice_fusion.2
  88.6 1.4 constant_dynamic-slice_fusion
  91.6 7.5 %collective-permute-start.2 = (f32[256,864]{0,1:T(8,128)S(1)}, f32[256,864]{0,1:T(8,128)S(1)}, u32[]{:S(2)}, u32[]{:S(2)}) collective-permute-start(f32[256,864]{0,1:T(8,128)S(1)} %convolution_add_fusion), channel_id=1, source_target_pairs={{0,1},{1,0},{2,3},{3,2},{4,5},{5,4},{6,7},{7,6},{8,9},{9,8},{10,11... | collective-permute-start | bytes 2654216 | tf_op jit(solution)/shard_map/ppermute | solution.py:84
  101.1 1.4 fusion.4
  102.6 2.1 %fusion.19 = f32[256,864]{0,1:T(8,128)S(1)} fusion(bf16[256,704]{1,0:T(8,128)(2,1)} %copy-done.1, bf16[704,864]{1,0:T(8,128)(2,1)} %collective-permute-done.1), kind=kOutput, calls=%fused_computation.42 | convolution fusion | flops 311427072 | bytes 2461696 | tf_op jit(solution)/shard_map/dot_general | solution.py:20
  104.7 1.6 convolution_add_fusion.2
  106.3 10.8 %collective-permute-start.4 = (f32[256,864]{0,1:T(8,128)}, f32[256,864]{0,1:T(8,128)S(1)}, u32[]{:S(2)}, u32[]{:S(2)}) collective-permute-start(f32[256,864]{0,1:T(8,128)} %convolution_add_fusion.2), channel_id=1, source_target_pairs={{0,1},{1,0},{2,3},{3,2},{4,5},{5,4},{6,7},{7,6},{8,9},{9,8},{10,11... | collective-permute-start | bytes 2654216 | tf_op jit(solution)/shard_map/ppermute | solution.py:84
  117.1 2.0 %fusion.18 = f32[256,864]{0,1:T(8,128)S(1)} fusion(bf16[256,704]{1,0:T(8,128)(2,1)S(1)} %get-tuple-element.23, bf16[704,864]{1,0:T(8,128)(2,1)} %collective-permute-done.1), kind=kOutput, calls=%fused_computation.41 | convolution fusion | flops 311427072 | bytes 2461696 | tf_op jit(solution)/shard_map/dot_general | solution.py:20
  120.9 19.1 %all_to_all.25 = bf16[16,32,864]{2,1,0:T(8,128)(2,1)S(1)} all-to-all(bf16[16,32,864]{2,1,0:T(8,128)(2,1)S(1)} %bitcast.42), channel_id=1, replica_groups=mesh['z'=16,'xh'=2,'xl'=2,'y'=4,'core'=2] {'xh','xl','y'}, dimensions={0} | all-to-all | bytes 1769472 | tf_op jit(solution)/shard_map/all_to_all | solution.py:91
  141.1 3.6 %all-to-all-start.4 = ((bf16[8,2,32,864]{3,2,1,0:T(8,128)(2,1)}), bf16[8,2,32,864]{3,2,1,0:T(8,128)(2,1)S(1)}, u32[]{:S(2)}, u32[]{:S(2)}) async-start(bf16[8,2,32,864]{3,2,1,0:T(8,128)(2,1)} %broadcast_in_dim.5), calls=%async_computation.4 | async-start | bytes 1835008 | tf_op jit(solution)/shard_map/all_to_all | solution.py:39
  144.7 3.6 %collective-permute-start.3 = (bf16[16,32,320]{2,1,0:T(8,128)(2,1)}, bf16[16,32,320]{2,1,0:T(8,128)(2,1)S(1)}, u32[]{:S(2)}, u32[]{:S(2)}) collective-permute-start(bf16[16,32,320]{2,1,0:T(8,128)(2,1)} %all-to-all-done.2), channel_id=1, source_target_pairs={{0,16},{16,0},{1,17},{17,1},{2,18},{18,2},{3,19},{19,3},{4,20},{20... | collective-permute-start | bytes 983048 | tf_op jit(solution)/shard_map/ppermute | solution.py:50
  148.3 6.4 %all-to-all-done.4 = bf16[8,2,32,864]{3,2,1,0:T(8,128)(2,1)S(1)} async-done(((bf16[8,2,32,864]{3,2,1,0:T(8,128)(2,1)}), bf16[8,2,32,864]{3,2,1,0:T(8,128)(2,1)S(1)}, u32[]{:S(2)}, u32[]{:S(2)}) %all-to-all-start.4) | async-done | bytes 884768 | tf_op jit(solution)/shard_map/all_to_all | solution.py:39
  155.2 7.7 %collective-permute-start.5 = (bf16[512,864]{0,1:T(8,128)(2,1)S(1)}, bf16[512,864]{0,1:T(8,128)(2,1)S(1)}, u32[]{:S(2)}, u32[]{:S(2)}) collective-permute-start(bf16[512,864]{0,1:T(8,128)(2,1)S(1)} %copy.18), channel_id=1, source_target_pairs={{0,1},{1,0},{2,3},{3,2},{4,5},{5,4},{6,7},{7,6},{8,9},{9,8},{10,11... | collective-permute-start | bytes 2654216 | tf_op jit(solution)/shard_map/ppermute | solution.py:97
  166.0 1.6 fusion.1
  (50 shorter events, 14.3 us)
Async XLA Ops:
  6.5 80.7 %all-gather.2.cloned.1.call-start = ((), (), s32[]{:S(2)}) async-start(), calls=%async_computation.5 | async-start | bytes 1949696 | tf_op jit(solution)/shard_map/all_gather | solution.py:55
  7.3 1.5 slice-start
  8.8 7.9 %copy-start.7 = (bf16[32,5120]{1,0:T(8,128)(2,1)S(1)}, bf16[32,5120]{1,0:T(8,128)(2,1)}, u32[]{:S(2)}) copy-start(bf16[32,5120]{1,0:T(8,128)(2,1)} %param.4) | copy-start | bytes 983044
  11.2 54.1 %collective-permute-start = (bf16[1024,864]{0,1:T(8,128)(2,1)}, bf16[1024,864]{0,1:T(8,128)(2,1)S(1)}, u32[]{:S(2)}, u32[]{:S(2)}) collective-permute-start(bf16[1024,864]{0,1:T(8,128)(2,1)} %copy.19), channel_id=1, source_target_pairs={{0,16},{16,0},{1,17},{17,1},{2,18},{18,2},{3,19},{19,3},{4,20},{20... | collective-permute-start | bytes 5308424 | tf_op jit(solution)/shard_map/ppermute | solution.py:50
  18.6 44.5 %all-to-all-start = ((bf16[4,32,1280]{2,1,0:T(8,128)(2,1)}), bf16[4,32,1280]{2,1,0:T(8,128)(2,1)S(1)}, u32[]{:S(2)}, u32[]{:S(2)}) async-start(bf16[4,32,1280]{2,1,0:T(8,128)(2,1)} %reshape.35), calls=%async_computation | async-start | bytes 655360 | tf_op jit(solution)/shard_map/all_to_all | solution.py:60
  22.1 1.5 copy-start.8
  65.3 12.1 %all-to-all-start.1 = ((f32[4,32,320]{2,1,0:T(8,128)}), f32[4,32,320]{2,1,0:T(8,128)S(1)}, u32[]{:S(2)}, u32[]{:S(2)}) async-start(f32[4,32,320]{2,1,0:T(8,128)} %fusion.6), calls=%async_computation.1 | async-start | bytes 393216 | tf_op jit(solution)/shard_map/all_to_all | solution.py:67
  71.7 30.8 %collective-permute-start.1 = (bf16[704,864]{1,0:T(8,128)(2,1)S(1)}, bf16[704,864]{1,0:T(8,128)(2,1)}, u32[]{:S(2)}, u32[]{:S(2)}) collective-permute-start(bf16[704,864]{1,0:T(8,128)(2,1)S(1)} %slice.88), channel_id=1, source_target_pairs={{0,16},{16,0},{1,17},{17,1},{2,18},{18,2},{3,19},{19,3},{4,20},{20... | collective-permute-start | bytes 3649544 | tf_op jit(solution)/shard_map/ppermute | solution.py:50
  78.3 24.3 %all-to-all-start.2 = ((bf16[16,32,320]{2,1,0:T(8,128)(2,1)}), bf16[16,32,320]{2,1,0:T(8,128)(2,1)}, u32[]{:S(2)}, u32[]{:S(2)}) async-start(bf16[16,32,320]{2,1,0:T(8,128)(2,1)} %broadcast_in_dim.4), calls=%async_computation.2 | async-start | bytes 786432 | tf_op jit(solution)/shard_map/all_to_all | solution.py:39
  87.3 2.8 %copy-start = (bf16[1728,864]{1,0:T(8,128)(2,1)S(1)}, bf16[1728,864]{1,0:T(8,128)(2,1)}, u32[]{:S(2)}) copy-start(bf16[1728,864]{1,0:T(8,128)(2,1)} %param.7) | copy-start | bytes 8957956
  88.6 2.3 %copy-start.1 = (bf16[256,704]{1,0:T(8,128)(2,1)}, bf16[256,704]{1,0:T(8,128)(2,1)S(1)}, u32[]{:S(2)}) copy-start(bf16[256,704]{1,0:T(8,128)(2,1)S(1)} %get-tuple-element.25) | copy-start | bytes 1081348
  90.1 0.9 copy-start.4
  90.1 9.0 %copy-start.2 = (bf16[256,1024]{1,0:T(8,128)(2,1)}, bf16[256,1024]{1,0:T(8,128)(2,1)S(1)}, u32[]{:S(2)}) copy-start(bf16[256,1024]{1,0:T(8,128)(2,1)S(1)} %get-tuple-element.22) | copy-start | bytes 1572868
  91.6 9.5 %collective-permute-start.2 = (f32[256,864]{0,1:T(8,128)S(1)}, f32[256,864]{0,1:T(8,128)S(1)}, u32[]{:S(2)}, u32[]{:S(2)}) collective-permute-start(f32[256,864]{0,1:T(8,128)S(1)} %convolution_add_fusion), channel_id=1, source_target_pairs={{0,1},{1,0},{2,3},{3,2},{4,5},{5,4},{6,7},{7,6},{8,9},{9,8},{10,11... | collective-permute-start | bytes 2654216 | tf_op jit(solution)/shard_map/ppermute | solution.py:84
  102.6 2.1 %copy-start.5 = (bf16[256,1024]{1,0:T(8,128)(2,1)S(1)}, bf16[256,1024]{1,0:T(8,128)(2,1)}, u32[]{:S(2)}) copy-start(bf16[256,1024]{1,0:T(8,128)(2,1)} %copy-done.4) | copy-start | bytes 1572868
  106.3 13.0 %collective-permute-start.4 = (f32[256,864]{0,1:T(8,128)}, f32[256,864]{0,1:T(8,128)S(1)}, u32[]{:S(2)}, u32[]{:S(2)}) collective-permute-start(f32[256,864]{0,1:T(8,128)} %convolution_add_fusion.2), channel_id=1, source_target_pairs={{0,1},{1,0},{2,3},{3,2},{4,5},{5,4},{6,7},{7,6},{8,9},{9,8},{10,11... | collective-permute-start | bytes 2654216 | tf_op jit(solution)/shard_map/ppermute | solution.py:84
  117.1 2.2 %copy-start.3 = (bf16[256,1024]{1,0:T(8,128)(2,1)S(1)}, bf16[256,1024]{1,0:T(8,128)(2,1)}, u32[]{:S(2)}) copy-start(bf16[256,1024]{1,0:T(8,128)(2,1)} %copy-done.2) | copy-start | bytes 1572868
  119.1 1.0 copy-start.6
  141.1 13.6 %all-to-all-start.4 = ((bf16[8,2,32,864]{3,2,1,0:T(8,128)(2,1)}), bf16[8,2,32,864]{3,2,1,0:T(8,128)(2,1)S(1)}, u32[]{:S(2)}, u32[]{:S(2)}) async-start(bf16[8,2,32,864]{3,2,1,0:T(8,128)(2,1)} %broadcast_in_dim.5), calls=%async_computation.4 | async-start | bytes 1835008 | tf_op jit(solution)/shard_map/all_to_all | solution.py:39
  144.7 19.5 %collective-permute-start.3 = (bf16[16,32,320]{2,1,0:T(8,128)(2,1)}, bf16[16,32,320]{2,1,0:T(8,128)(2,1)S(1)}, u32[]{:S(2)}, u32[]{:S(2)}) collective-permute-start(bf16[16,32,320]{2,1,0:T(8,128)(2,1)} %all-to-all-done.2), channel_id=1, source_target_pairs={{0,16},{16,0},{1,17},{17,1},{2,18},{18,2},{3,19},{19,3},{4,20},{20... | collective-permute-start | bytes 983048 | tf_op jit(solution)/shard_map/ppermute | solution.py:50
  155.2 10.8 %collective-permute-start.5 = (bf16[512,864]{0,1:T(8,128)(2,1)S(1)}, bf16[512,864]{0,1:T(8,128)(2,1)S(1)}, u32[]{:S(2)}, u32[]{:S(2)}) collective-permute-start(bf16[512,864]{0,1:T(8,128)(2,1)S(1)} %copy.18), channel_id=1, source_target_pairs={{0,1},{1,0},{2,3},{3,2},{4,5},{5,4},{6,7},{7,6},{8,9},{9,8},{10,11... | collective-permute-start | bytes 2654216 | tf_op jit(solution)/shard_map/ppermute | solution.py:97
Sparse Core Ops, SparseCore 0:
  9.4 75.7 all-gather.1

commit v5 on v4

--- a/solution.py
+++ b/solution.py
@@ -11,7 +11,7 @@
 COL = ("xl", "y", "core")
 SWAP = [(0, 1), (1, 0)]
 BF, F32 = jnp.bfloat16, jnp.float32
-SPLIT = 1024
+SPLIT = 944
 
 PARITY = [[p + 2 * k for k in range(NZ // 2)] for p in range(2)]
 QUADS = [[(2 * k + i) * NXH + h for i in range(2) for h in range(NXH)] for k in range(NZ // 2)]
@@ -80,13 +80,17 @@
 
     mine, theirs = tie(rows_of(seq), rows_of(1 - seq))
 
-    def products(first, second):
-        added = lax.ppermute(dot(theirs[0], first) + dot(theirs[1], second), "core", SWAP)
-        return (dot(mine[0], first) + dot(mine[1], second) + added).astype(BF)
+    def rounded(second, started):
+        theirs_first, mine_first = started
+        added = lax.ppermute(theirs_first + dot(theirs[1], second), "core", SWAP)
+        return (mine_first + dot(mine[1], second) + added).astype(BF)
 
-    sums = products(first, second)
-    second_other, sums, acts = tie(second_other, sums, acts)
-    sums = in_order(sums, products(first_other, second_other))
+    def start(first):
+        return dot(theirs[0], first), dot(mine[0], first)
+
+    sums = rounded(second, start(first))
+    second_other, sums, acts, started = tie(second_other, sums, acts, start(first_other))
+    sums = in_order(sums, rounded(second_other, started))
     sums = jnp.stack(sums).reshape(NXH * n, half // n, cols)
     sums = lax.all_to_all(sums, ("xh", "xl", "y"), 0, 0)
     acts = jnp.stack(in_order(acts, swap(acts)), axis=1).reshape(SEQS * SEQ_LEN, act_cols)

time: 176 us -> 174 us (0.989)
  starting transfers between devices: 62.4 us -> 56.2 us
  blocking collectives: 58.7 us -> 61.3 us
    unnamed x21 -> x14, local copies, waits for them, and re-layouts: 4.01 us -> 0.22 us
    slice x1 -> x2, local copies, waits for them, and re-layouts: 1.44 us -> 4.31 us  [local(): first, second = (grad_basis[:SPLIT], grad_basis[SPLIT:])]
    ppermute x2, starting transfers between devices: 18.2 us -> 15.5 us  [rounded(): added = lax.ppermute(theirs_first + dot(theirs[1], second), 'core', SWAP)]
    all_to_all x1, blocking collectives: 19.1 us -> 21.7 us  [local(): sums = lax.all_to_all(sums, ('xh', 'xl', 'y'), 0, 0)]
  transfers between devices with their start and end apart: 11 -> 11, of which waited for: 5 -> 5; matrix products, arithmetic and copies ran while one was open for 11% -> 14% of each run, Pallas kernels for 0% -> 0%
where the time goes in v5:
time: 174 us; the launch traced here: 173 us
  blocking collectives  61.3 us (35%)
  starting transfers between devices  56.2 us (32%)
  matrix products  15.4 us (9%)
  between operations  13.7 us (8%)
  local copies, waits for them, and re-layouts  12.6 us (7%)
  waiting for transfers between devices  10.7 us (6%)
  other arithmetic  2.77 us (2%)
    all_gather x1, blocking collectives, local(): lax.all_gather(act_basis, 'z', axis=0, tiled=True, axis_index_groups=PARITY)  39.6 us
    all_to_all x1, blocking collectives, local(): sums = lax.all_to_all(sums, ('xh', 'xl', 'y'), 0, 0)  21.7 us
    ppermute x2, starting transfers between devices, rounded(): added = lax.ppermute(theirs_first + dot(theirs[1], second), 'core', SWAP)  15.5 us
    ppermute x3, starting transfers between devices, swap(): return lax.ppermute(x, 'xh', SWAP)  13.5 us
    dot_general x9, matrix products, dot(): return jnp.dot(a, b, preferred_element_type=F32)  13.2 us
    all_to_all x2, starting transfers between devices, spread(): return lax.all_to_all(jnp.broadcast_to(x[None], (n,) + x.shape), axes, 0, 0)  11.1 us
    all_to_all x2, waiting for transfers between devices, spread(): return lax.all_to_all(jnp.broadcast_to(x[None], (n,) + x.shape), axes, 0, 0)  7.26 us
    ppermute x1, starting transfers between devices, local(): rest = lax.ppermute(own, 'core', SWAP)  6.82 us
  transfers between devices with their start and end apart: 11, of which 5 were waited for; matrix products, arithmetic and copies ran while one was open for 14% of the time, Pallas kernels for 0%

profile of v5, /device:TPU:1, one launch (start us, length us, event | category | flops | bytes accessed | tf_op | source)
XLA Modules:
  0.0 172.7 jit_solution(9584863051285105341)
XLA Ops:
  7.3 2.8 %slice.89 = bf16[944,864]{1,0:T(8,128)(2,1)} slice(bf16[1728,864]{1,0:T(8,128)(2,1)} %param.7), slice={[0:944], [0:864]} | slice | bytes 3262464 | tf_op jit(solution)/shard_map/slice | solution.py:61
  10.1 5.5 %collective-permute-start = (bf16[944,864]{1,0:T(8,128)(2,1)}, bf16[944,864]{1,0:T(8,128)(2,1)S(1)}, u32[]{:S(2)}, u32[]{:S(2)}) collective-permute-start(bf16[944,864]{1,0:T(8,128)(2,1)} %slice.89), channel_id=1, source_target_pairs={{0,16},{16,0},{1,17},{17,1},{2,18},{18,2},{3,19},{19,3},{4,20},{20... | collective-permute-start | bytes 4893704 | tf_op jit(solution)/shard_map/ppermute | solution.py:50
  17.5 3.5 %all-to-all-start = ((bf16[4,32,1280]{2,1,0:T(8,128)(2,1)}), bf16[4,32,1280]{2,1,0:T(8,128)(2,1)S(1)}, u32[]{:S(2)}, u32[]{:S(2)}) async-start(bf16[4,32,1280]{2,1,0:T(8,128)(2,1)} %reshape.35), calls=%async_computation | async-start | bytes 655360 | tf_op jit(solution)/shard_map/all_to_all | solution.py:60
  21.0 1.5 slice.88
  22.5 39.6 %all_gather.6 = bf16[1280,320]{1,0:T(8,128)(2,1)} all-gather(bf16[160,320]{1,0:T(8,128)(2,1)S(1)} %copy-done.6), channel_id=1, replica_groups={{0,64,128,192,256,320,384,448},{32,96,160,224,288,352,416,480},{1,65,12..., dimensions={0}, use_global_device_ids=true | all-gather | bytes 921600 | tf_op jit(solution)/shard_map/all_gather | solution.py:63
  62.1 2.2 %fusion.4 = f32[4,32,320]{2,1,0:T(8,128)} fusion(bf16[4,32,1280]{2,1,0:T(8,128)(2,1)S(1)} %all-to-all-done, bf16[1280,320]{1,0:T(8,128)(2,1)} %all_gather.6), kind=kOutput, calls=%fused_computation.8 | convolution fusion | flops 104857600 | bytes 1310720 | tf_op jit(solution)/shard_map/dot_general | solution.py:20
  64.3 5.8 %all-to-all-start.1 = ((f32[4,32,320]{2,1,0:T(8,128)}), f32[4,32,320]{2,1,0:T(8,128)S(1)}, u32[]{:S(2)}, u32[]{:S(2)}) async-start(f32[4,32,320]{2,1,0:T(8,128)} %fusion.4), calls=%async_computation.1 | async-start | bytes 393216 | tf_op jit(solution)/shard_map/all_to_all | solution.py:67
  70.1 4.9 %collective-permute-start.1 = (bf16[784,864]{1,0:T(8,128)(2,1)S(1)}, bf16[784,864]{1,0:T(8,128)(2,1)}, u32[]{:S(2)}, u32[]{:S(2)}) collective-permute-start(bf16[784,864]{1,0:T(8,128)(2,1)S(1)} %slice.88), channel_id=1, source_target_pairs={{0,16},{16,0},{1,17},{17,1},{2,18},{18,2},{3,19},{19,3},{4,20},{20... | collective-permute-start | bytes 4064264 | tf_op jit(solution)/shard_map/ppermute | solution.py:50
  76.7 7.6 %all-to-all-start.2 = ((bf16[16,32,320]{2,1,0:T(8,128)(2,1)}), bf16[16,32,320]{2,1,0:T(8,128)(2,1)}, u32[]{:S(2)}, u32[]{:S(2)}) async-start(bf16[16,32,320]{2,1,0:T(8,128)(2,1)} %broadcast_in_dim.4), calls=%async_computation.2 | async-start | bytes 786432 | tf_op jit(solution)/shard_map/all_to_all | solution.py:39
  84.7 1.8 %constant_dynamic-slice_fusion.2 = (bf16[256,784]{1,0:T(8,128)(2,1)S(1)}, bf16[256,784]{1,0:T(8,128)(2,1)S(1)}) fusion(bf16[512,1728]{1,0:T(8,128)(2,1)} %all-gather.2.cloned.1.call-done, s32[]{:T(128)S(6)} %select_n.40, s32[]{:T(128)S(6)} %select_n.39), kind=kLoop, calls=%fused_computation.32 | loop fusion | bytes 1605640 | tf_op jit(solution)/shard_map/dynamic_slice | solution.py:77
  86.5 1.4 constant_dynamic-slice_fusion
  89.5 12.0 %collective-permute-start.2 = (f32[256,864]{0,1:T(8,128)S(1)}, f32[256,864]{0,1:T(8,128)S(1)}, u32[]{:S(2)}, u32[]{:S(2)}) collective-permute-start(f32[256,864]{0,1:T(8,128)S(1)} %convolution_add_fusion), channel_id=1, source_target_pairs={{0,1},{1,0},{2,3},{3,2},{4,5},{5,4},{6,7},{7,6},{8,9},{9,8},{10,11... | collective-permute-start | bytes 2654216 | tf_op jit(solution)/shard_map/ppermute | solution.py:85
  101.6 1.7 %fusion.16 = f32[256,864]{0,1:T(8,128)} fusion(bf16[256,944]{1,0:T(8,128)(2,1)S(1)} %get-tuple-element.26, bf16[944,864]{1,0:T(8,128)(2,1)S(1)} %collective-permute-done), kind=kOutput, calls=%fused_computation.38 | convolution fusion | flops 417595392 | bytes 2999296 | tf_op jit(solution)/shard_map/dot_general | solution.py:20
  103.3 1.8 %fusion.17 = f32[256,864]{0,1:T(8,128)} fusion(bf16[256,944]{1,0:T(8,128)(2,1)S(1)} %get-tuple-element.24, bf16[944,864]{1,0:T(8,128)(2,1)S(1)} %collective-permute-done), kind=kOutput, calls=%fused_computation.39 | convolution fusion | flops 417595392 | bytes 2999296 | tf_op jit(solution)/shard_map/dot_general | solution.py:20
  107.0 2.2 %fusion.19 = f32[256,864]{0,1:T(8,128)S(1)} fusion(bf16[256,784]{1,0:T(8,128)(2,1)S(1)} %copy-done.1, bf16[784,864]{1,0:T(8,128)(2,1)} %collective-permute-done.1), kind=kOutput, calls=%fused_computation.41 | convolution fusion | flops 346816512 | bytes 2640896 | tf_op jit(solution)/shard_map/dot_general | solution.py:20
  110.2 3.4 %collective-permute-start.4 = (f32[256,864]{0,1:T(8,128)}, f32[256,864]{0,1:T(8,128)S(1)}, u32[]{:S(2)}, u32[]{:S(2)}) collective-permute-start(f32[256,864]{0,1:T(8,128)} %add.113), channel_id=1, source_target_pairs={{0,1},{1,0},{2,3},{3,2},{4,5},{5,4},{6,7},{7,6},{8,9},{9,8},{10,11... | collective-permute-start | bytes 2654216 | tf_op jit(solution)/shard_map/ppermute | solution.py:85
  113.6 2.1 %fusion.18 = f32[256,864]{0,1:T(8,128)S(1)} fusion(bf16[256,784]{1,0:T(8,128)(2,1)S(1)} %get-tuple-element.25, bf16[784,864]{1,0:T(8,128)(2,1)} %collective-permute-done.1), kind=kOutput, calls=%fused_computation.40 | convolution fusion | flops 346816512 | bytes 2640896 | tf_op jit(solution)/shard_map/dot_general | solution.py:20
  116.9 21.7 %all_to_all.25 = bf16[16,32,864]{2,1,0:T(8,128)(2,1)S(1)} all-to-all(bf16[16,32,864]{2,1,0:T(8,128)(2,1)S(1)} %bitcast.42), channel_id=1, replica_groups=mesh['z'=16,'xh'=2,'xl'=2,'y'=4,'core'=2] {'xh','xl','y'}, dimensions={0} | all-to-all | bytes 1769472 | tf_op jit(solution)/shard_map/all_to_all | solution.py:95
  139.7 3.6 %all-to-all-start.4 = ((bf16[8,2,32,864]{3,2,1,0:T(8,128)(2,1)}), bf16[8,2,32,864]{3,2,1,0:T(8,128)(2,1)S(1)}, u32[]{:S(2)}, u32[]{:S(2)}) async-start(bf16[8,2,32,864]{3,2,1,0:T(8,128)(2,1)} %broadcast_in_dim.5), calls=%async_computation.4 | async-start | bytes 1835008 | tf_op jit(solution)/shard_map/all_to_all | solution.py:39
  143.3 3.2 %collective-permute-start.3 = (bf16[16,32,320]{2,1,0:T(8,128)(2,1)}, bf16[16,32,320]{2,1,0:T(8,128)(2,1)S(1)}, u32[]{:S(2)}, u32[]{:S(2)}) collective-permute-start(bf16[16,32,320]{2,1,0:T(8,128)(2,1)} %all-to-all-done.2), channel_id=1, source_target_pairs={{0,16},{16,0},{1,17},{17,1},{2,18},{18,2},{3,19},{19,3},{4,20},{20... | collective-permute-start | bytes 983048 | tf_op jit(solution)/shard_map/ppermute | solution.py:50
  146.5 7.3 %all-to-all-done.4 = bf16[8,2,32,864]{3,2,1,0:T(8,128)(2,1)S(1)} async-done(((bf16[8,2,32,864]{3,2,1,0:T(8,128)(2,1)}), bf16[8,2,32,864]{3,2,1,0:T(8,128)(2,1)S(1)}, u32[]{:S(2)}, u32[]{:S(2)}) %all-to-all-start.4) | async-done | bytes 884768 | tf_op jit(solution)/shard_map/all_to_all | solution.py:39
  154.3 6.8 %collective-permute-start.5 = (bf16[512,864]{0,1:T(8,128)(2,1)S(1)}, bf16[512,864]{0,1:T(8,128)(2,1)S(1)}, u32[]{:S(2)}, u32[]{:S(2)}) collective-permute-start(bf16[512,864]{0,1:T(8,128)(2,1)S(1)} %copy.16), channel_id=1, source_target_pairs={{0,1},{1,0},{2,3},{3,2},{4,5},{5,4},{6,7},{7,6},{8,9},{9,8},{10,11... | collective-permute-start | bytes 2654216 | tf_op jit(solution)/shard_map/ppermute | solution.py:101
  161.1 1.4 collective-permute-done.3
  164.2 1.6 fusion.1
  (46 shorter events, 13.7 us)
Async XLA Ops:
  6.5 78.1 %all-gather.2.cloned.1.call-start = ((), (), s32[]{:S(2)}) async-start(), calls=%async_computation.5 | async-start | bytes 1949696 | tf_op jit(solution)/shard_map/all_gather | solution.py:55
  7.3 8.3 %copy-start.5 = (bf16[32,5120]{1,0:T(8,128)(2,1)S(1)}, bf16[32,5120]{1,0:T(8,128)(2,1)}, u32[]{:S(2)}) copy-start(bf16[32,5120]{1,0:T(8,128)(2,1)} %param.4) | copy-start | bytes 983044
  10.1 54.2 %collective-permute-start = (bf16[944,864]{1,0:T(8,128)(2,1)}, bf16[944,864]{1,0:T(8,128)(2,1)S(1)}, u32[]{:S(2)}, u32[]{:S(2)}) collective-permute-start(bf16[944,864]{1,0:T(8,128)(2,1)} %slice.89), channel_id=1, source_target_pairs={{0,16},{16,0},{1,17},{17,1},{2,18},{18,2},{3,19},{19,3},{4,20},{20... | collective-permute-start | bytes 4893704 | tf_op jit(solution)/shard_map/ppermute | solution.py:50
  17.5 44.6 %all-to-all-start = ((bf16[4,32,1280]{2,1,0:T(8,128)(2,1)}), bf16[4,32,1280]{2,1,0:T(8,128)(2,1)S(1)}, u32[]{:S(2)}, u32[]{:S(2)}) async-start(bf16[4,32,1280]{2,1,0:T(8,128)(2,1)} %reshape.35), calls=%async_computation | async-start | bytes 655360 | tf_op jit(solution)/shard_map/all_to_all | solution.py:60
  21.0 1.5 copy-start.6
  64.3 11.6 %all-to-all-start.1 = ((f32[4,32,320]{2,1,0:T(8,128)}), f32[4,32,320]{2,1,0:T(8,128)S(1)}, u32[]{:S(2)}, u32[]{:S(2)}) async-start(f32[4,32,320]{2,1,0:T(8,128)} %fusion.4), calls=%async_computation.1 | async-start | bytes 393216 | tf_op jit(solution)/shard_map/all_to_all | solution.py:67
  70.1 36.6 %collective-permute-start.1 = (bf16[784,864]{1,0:T(8,128)(2,1)S(1)}, bf16[784,864]{1,0:T(8,128)(2,1)}, u32[]{:S(2)}, u32[]{:S(2)}) collective-permute-start(bf16[784,864]{1,0:T(8,128)(2,1)S(1)} %slice.88), channel_id=1, source_target_pairs={{0,16},{16,0},{1,17},{17,1},{2,18},{18,2},{3,19},{19,3},{4,20},{20... | collective-permute-start | bytes 4064264 | tf_op jit(solution)/shard_map/ppermute | solution.py:50
  76.7 30.1 %all-to-all-start.2 = ((bf16[16,32,320]{2,1,0:T(8,128)(2,1)}), bf16[16,32,320]{2,1,0:T(8,128)(2,1)}, u32[]{:S(2)}, u32[]{:S(2)}) async-start(bf16[16,32,320]{2,1,0:T(8,128)(2,1)} %broadcast_in_dim.4), calls=%async_computation.2 | async-start | bytes 786432 | tf_op jit(solution)/shard_map/all_to_all | solution.py:39
  84.7 3.3 %copy-start.4 = (bf16[1728,864]{1,0:T(8,128)(2,1)S(1)}, bf16[1728,864]{1,0:T(8,128)(2,1)}, u32[]{:S(2)}) copy-start(bf16[1728,864]{1,0:T(8,128)(2,1)} %param.7) | copy-start | bytes 8957956
  86.5 2.3 %copy-start = (bf16[256,784]{1,0:T(8,128)(2,1)}, bf16[256,784]{1,0:T(8,128)(2,1)S(1)}, u32[]{:S(2)}) copy-start(bf16[256,784]{1,0:T(8,128)(2,1)S(1)} %get-tuple-element.27) | copy-start | bytes 1204228
  89.5 16.4 %collective-permute-start.2 = (f32[256,864]{0,1:T(8,128)S(1)}, f32[256,864]{0,1:T(8,128)S(1)}, u32[]{:S(2)}, u32[]{:S(2)}) collective-permute-start(f32[256,864]{0,1:T(8,128)S(1)} %convolution_add_fusion), channel_id=1, source_target_pairs={{0,1},{1,0},{2,3},{3,2},{4,5},{5,4},{6,7},{7,6},{8,9},{9,8},{10,11... | collective-permute-start | bytes 2654216 | tf_op jit(solution)/shard_map/ppermute | solution.py:85
  105.9 1.0 copy-start.1
  106.8 2.4 %copy-start.3 = (f32[256,864]{0,1:T(8,128)S(1)}, f32[256,864]{0,1:T(8,128)}, u32[]{:S(2)}) copy-start(f32[256,864]{0,1:T(8,128)} %fusion.16) | copy-start | bytes 2654212
  110.2 5.7 %copy-start.2 = (f32[256,864]{0,1:T(8,128)S(1)}, f32[256,864]{0,1:T(8,128)}, u32[]{:S(2)}) copy-start(f32[256,864]{0,1:T(8,128)} %fusion.17) | copy-start | bytes 2654212
  110.2 5.7 %collective-permute-start.4 = (f32[256,864]{0,1:T(8,128)}, f32[256,864]{0,1:T(8,128)S(1)}, u32[]{:S(2)}, u32[]{:S(2)}) collective-permute-start(f32[256,864]{0,1:T(8,128)} %add.113), channel_id=1, source_target_pairs={{0,1},{1,0},{2,3},{3,2},{4,5},{5,4},{6,7},{7,6},{8,9},{9,8},{10,11... | collective-permute-start | bytes 2654216 | tf_op jit(solution)/shard_map/ppermute | solution.py:85
  139.7 14.0 %all-to-all-start.4 = ((bf16[8,2,32,864]{3,2,1,0:T(8,128)(2,1)}), bf16[8,2,32,864]{3,2,1,0:T(8,128)(2,1)S(1)}, u32[]{:S(2)}, u32[]{:S(2)}) async-start(bf16[8,2,32,864]{3,2,1,0:T(8,128)(2,1)} %broadcast_in_dim.5), calls=%async_computation.4 | async-start | bytes 1835008 | tf_op jit(solution)/shard_map/all_to_all | solution.py:39
  143.3 19.2 %collective-permute-start.3 = (bf16[16,32,320]{2,1,0:T(8,128)(2,1)}, bf16[16,32,320]{2,1,0:T(8,128)(2,1)S(1)}, u32[]{:S(2)}, u32[]{:S(2)}) collective-permute-start(bf16[16,32,320]{2,1,0:T(8,128)(2,1)} %all-to-all-done.2), channel_id=1, source_target_pairs={{0,16},{16,0},{1,17},{17,1},{2,18},{18,2},{3,19},{19,3},{4,20},{20... | collective-permute-start | bytes 983048 | tf_op jit(solution)/shard_map/ppermute | solution.py:50
  154.3 10.0 %collective-permute-start.5 = (bf16[512,864]{0,1:T(8,128)(2,1)S(1)}, bf16[512,864]{0,1:T(8,128)(2,1)S(1)}, u32[]{:S(2)}, u32[]{:S(2)}) collective-permute-start(bf16[512,864]{0,1:T(8,128)(2,1)S(1)} %copy.16), channel_id=1, source_target_pairs={{0,1},{1,0},{2,3},{3,2},{4,5},{5,4},{6,7},{7,6},{8,9},{9,8},{10,11... | collective-permute-start | bytes 2654216 | tf_op jit(solution)/shard_map/ppermute | solution.py:101
Sparse Core Ops, SparseCore 0:
  9.4 75.1 all-gather.1

commit v6 on v5

--- a/solution.py
+++ b/solution.py
@@ -68,6 +68,7 @@
     second_other = swap(second)
     acts = total(acts).astype(BF)
     seq, acts = tie(core, acts)
+    acts = jnp.concatenate([acts[: tokens // 2], acts[tokens // 2 :]], axis=1)
     acts = spread(acts, "z", NZ)
 
     half, hidden = tokens * NZ // SEQS, gradients.shape[1]
@@ -93,7 +94,9 @@
     sums = in_order(sums, rounded(second_other, started))
     sums = jnp.stack(sums).reshape(NXH * n, half // n, cols)
     sums = lax.all_to_all(sums, ("xh", "xl", "y"), 0, 0)
-    acts = jnp.stack(in_order(acts, swap(acts)), axis=1).reshape(SEQS * SEQ_LEN, act_cols)
+    acts = jnp.stack(in_order(acts, swap(acts)), axis=1)
+    acts = jnp.concatenate([acts[..., :act_cols], acts[..., act_cols:]], axis=2)
+    acts = acts.reshape(SEQS * SEQ_LEN, act_cols)
 
     sums = sums.reshape(NXH, n, half // n, cols)
     own = jnp.stack([total(sums[h]).astype(BF) for h in range(NXH)])

time: 174 us -> 173 us (level)
  waiting for transfers between devices: 10.7 us -> 8.25 us
  transfers between devices with their start and end apart: 11 -> 11, of which waited for: 5 -> 4; matrix products, arithmetic and copies ran while one was open for 14% -> 14% of each run, Pallas kernels for 0% -> 0%
where the time goes in v6:
time: 173 us; the launch traced here: 171 us
  blocking collectives  61.4 us (35%)
  starting transfers between devices  57 us (33%)
  matrix products  15.3 us (9%)
  between operations  13.8 us (8%)
  local copies, waits for them, and re-layouts  12.6 us (7%)
  waiting for transfers between devices  8.25 us (5%)
  other arithmetic  2.93 us (2%)
    all_gather x1, blocking collectives, local(): lax.all_gather(act_basis, 'z', axis=0, tiled=True, axis_index_groups=PARITY)  39.9 us
    all_to_all x1, blocking collectives, local(): sums = lax.all_to_all(sums, ('xh', 'xl', 'y'), 0, 0)  21.5 us
    ppermute x2, starting transfers between devices, rounded(): added = lax.ppermute(theirs_first + dot(theirs[1], second), 'core', SWAP)  14.6 us
    ppermute x3, starting transfers between devices, swap(): return lax.ppermute(x, 'xh', SWAP)  14 us
    dot_general x9, matrix products, dot(): return jnp.dot(a, b, preferred_element_type=F32)  13.2 us
    all_to_all x2, starting transfers between devices, spread(): return lax.all_to_all(jnp.broadcast_to(x[None], (n,) + x.shape), axes, 0, 0)  12 us
    ppermute x1, starting transfers between devices, local(): rest = lax.ppermute(own, 'core', SWAP)  7.83 us
    all_to_all x2, waiting for transfers between devices, spread(): return lax.all_to_all(jnp.broadcast_to(x[None], (n,) + x.shape), axes, 0, 0)  6.29 us
  transfers between devices with their start and end apart: 11, of which 4 were waited for; matrix products, arithmetic and copies ran while one was open for 14% of the time, Pallas kernels for 0%

profile of v6, /device:TPU:1, one launch (start us, length us, event | category | flops | bytes accessed | tf_op | source)
XLA Modules:
  0.0 171.2 jit_solution(14044586357430393514)
XLA Ops:
  7.3 2.8 %slice.101 = bf16[944,864]{1,0:T(8,128)(2,1)} slice(bf16[1728,864]{1,0:T(8,128)(2,1)} %param.7), slice={[0:944], [0:864]} | slice | bytes 3262464 | tf_op jit(solution)/shard_map/slice | solution.py:61
  10.1 5.5 %collective-permute-start = (bf16[944,864]{1,0:T(8,128)(2,1)}, bf16[944,864]{1,0:T(8,128)(2,1)S(1)}, u32[]{:S(2)}, u32[]{:S(2)}) collective-permute-start(bf16[944,864]{1,0:T(8,128)(2,1)} %slice.101), channel_id=1, source_target_pairs={{0,16},{16,0},{1,17},{17,1},{2,18},{18,2},{3,19},{19,3},{4,20},{20... | collective-permute-start | bytes 4893704 | tf_op jit(solution)/shard_map/ppermute | solution.py:50
  16.2 1.3 reshape.35
  17.5 3.6 %all-to-all-start = ((bf16[4,32,1280]{2,1,0:T(8,128)(2,1)}), bf16[4,32,1280]{2,1,0:T(8,128)(2,1)S(1)}, u32[]{:S(2)}, u32[]{:S(2)}) async-start(bf16[4,32,1280]{2,1,0:T(8,128)(2,1)} %reshape.35), calls=%async_computation | async-start | bytes 655360 | tf_op jit(solution)/shard_map/all_to_all | solution.py:60
  21.1 1.5 slice.100
  22.6 39.9 %all_gather.6 = bf16[1280,320]{1,0:T(8,128)(2,1)} all-gather(bf16[160,320]{1,0:T(8,128)(2,1)S(1)} %copy-done.6), channel_id=1, replica_groups={{0,64,128,192,256,320,384,448},{32,96,160,224,288,352,416,480},{1,65,12..., dimensions={0}, use_global_device_ids=true | all-gather | bytes 921600 | tf_op jit(solution)/shard_map/all_gather | solution.py:63
  62.5 2.2 %fusion.4 = f32[4,32,320]{2,1,0:T(8,128)} fusion(bf16[4,32,1280]{2,1,0:T(8,128)(2,1)S(1)} %all-to-all-done, bf16[1280,320]{1,0:T(8,128)(2,1)} %all_gather.6), kind=kOutput, calls=%fused_computation.8 | convolution fusion | flops 104857600 | bytes 1310720 | tf_op jit(solution)/shard_map/dot_general | solution.py:20
  64.7 5.0 %all-to-all-start.1 = ((f32[4,32,320]{2,1,0:T(8,128)}), f32[4,32,320]{2,1,0:T(8,128)S(1)}, u32[]{:S(2)}, u32[]{:S(2)}) async-start(f32[4,32,320]{2,1,0:T(8,128)} %fusion.4), calls=%async_computation.1 | async-start | bytes 393216 | tf_op jit(solution)/shard_map/all_to_all | solution.py:67
  69.7 4.9 %collective-permute-start.1 = (bf16[784,864]{1,0:T(8,128)(2,1)S(1)}, bf16[784,864]{1,0:T(8,128)(2,1)}, u32[]{:S(2)}, u32[]{:S(2)}) collective-permute-start(bf16[784,864]{1,0:T(8,128)(2,1)S(1)} %slice.100), channel_id=1, source_target_pairs={{0,16},{16,0},{1,17},{17,1},{2,18},{18,2},{3,19},{19,3},{4,20},{20... | collective-permute-start | bytes 4064264 | tf_op jit(solution)/shard_map/ppermute | solution.py:50
  76.1 8.4 %all-to-all-start.2 = ((bf16[16,16,640]{2,1,0:T(8,128)(2,1)}), bf16[16,16,640]{2,1,0:T(8,128)(2,1)}, u32[]{:S(2)}, u32[]{:S(2)}) async-start(bf16[16,16,640]{2,1,0:T(8,128)(2,1)} %broadcast_in_dim.4), calls=%async_computation.2 | async-start | bytes 655360 | tf_op jit(solution)/shard_map/all_to_all | solution.py:39
  84.6 1.8 %constant_dynamic-slice_fusion.2 = (bf16[256,784]{1,0:T(8,128)(2,1)S(1)}, bf16[256,784]{1,0:T(8,128)(2,1)S(1)}) fusion(bf16[512,1728]{1,0:T(8,128)(2,1)} %all-gather.2.cloned.1.call-done, s32[]{:T(128)S(6)} %select_n.40, s32[]{:T(128)S(6)} %select_n.39), kind=kLoop, calls=%fused_computation.37 | loop fusion | bytes 1605640 | tf_op jit(solution)/shard_map/dynamic_slice | solution.py:78
  86.4 1.4 constant_dynamic-slice_fusion
  89.5 12.5 %collective-permute-start.2 = (f32[256,864]{0,1:T(8,128)S(1)}, f32[256,864]{0,1:T(8,128)S(1)}, u32[]{:S(2)}, u32[]{:S(2)}) collective-permute-start(f32[256,864]{0,1:T(8,128)S(1)} %convolution_add_fusion), channel_id=1, source_target_pairs={{0,1},{1,0},{2,3},{3,2},{4,5},{5,4},{6,7},{7,6},{8,9},{9,8},{10,11... | collective-permute-start | bytes 2654216 | tf_op jit(solution)/shard_map/ppermute | solution.py:86
  102.0 1.7 %fusion.19 = f32[256,864]{0,1:T(8,128)} fusion(bf16[256,944]{1,0:T(8,128)(2,1)S(1)} %get-tuple-element.26, bf16[944,864]{1,0:T(8,128)(2,1)S(1)} %collective-permute-done), kind=kOutput, calls=%fused_computation.44 | convolution fusion | flops 417595392 | bytes 2999296 | tf_op jit(solution)/shard_map/dot_general | solution.py:20
  103.7 1.8 %fusion.20 = f32[256,864]{0,1:T(8,128)} fusion(bf16[256,944]{1,0:T(8,128)(2,1)S(1)} %get-tuple-element.24, bf16[944,864]{1,0:T(8,128)(2,1)S(1)} %collective-permute-done), kind=kOutput, calls=%fused_computation.45 | convolution fusion | flops 417595392 | bytes 2999296 | tf_op jit(solution)/shard_map/dot_general | solution.py:20
  107.3 2.2 %fusion.22 = f32[256,864]{0,1:T(8,128)S(1)} fusion(bf16[256,784]{1,0:T(8,128)(2,1)S(1)} %copy-done.1, bf16[784,864]{1,0:T(8,128)(2,1)} %collective-permute-done.1), kind=kOutput, calls=%fused_computation.47 | convolution fusion | flops 346816512 | bytes 2640896 | tf_op jit(solution)/shard_map/dot_general | solution.py:20
  110.5 2.2 %collective-permute-start.4 = (f32[256,864]{0,1:T(8,128)}, f32[256,864]{0,1:T(8,128)S(1)}, u32[]{:S(2)}, u32[]{:S(2)}) collective-permute-start(f32[256,864]{0,1:T(8,128)} %add.113), channel_id=1, source_target_pairs={{0,1},{1,0},{2,3},{3,2},{4,5},{5,4},{6,7},{7,6},{8,9},{9,8},{10,11... | collective-permute-start | bytes 2654216 | tf_op jit(solution)/shard_map/ppermute | solution.py:86
  112.7 2.1 %fusion.21 = f32[256,864]{0,1:T(8,128)S(1)} fusion(bf16[256,784]{1,0:T(8,128)(2,1)S(1)} %get-tuple-element.25, bf16[784,864]{1,0:T(8,128)(2,1)} %collective-permute-done.1), kind=kOutput, calls=%fused_computation.46 | convolution fusion | flops 346816512 | bytes 2640896 | tf_op jit(solution)/shard_map/dot_general | solution.py:20
  116.2 21.5 %all_to_all.25 = bf16[16,32,864]{2,1,0:T(8,128)(2,1)S(1)} all-to-all(bf16[16,32,864]{2,1,0:T(8,128)(2,1)S(1)} %bitcast.42), channel_id=1, replica_groups=mesh['z'=16,'xh'=2,'xl'=2,'y'=4,'core'=2] {'xh','xl','y'}, dimensions={0} | all-to-all | bytes 1769472 | tf_op jit(solution)/shard_map/all_to_all | solution.py:96
  138.8 3.6 %all-to-all-start.4 = ((bf16[8,2,32,864]{3,2,1,0:T(8,128)(2,1)}), bf16[8,2,32,864]{3,2,1,0:T(8,128)(2,1)S(1)}, u32[]{:S(2)}, u32[]{:S(2)}) async-start(bf16[8,2,32,864]{3,2,1,0:T(8,128)(2,1)} %broadcast_in_dim.5), calls=%async_computation.4 | async-start | bytes 1835008 | tf_op jit(solution)/shard_map/all_to_all | solution.py:39
  142.4 3.7 %collective-permute-start.3 = (bf16[16,16,640]{2,1,0:T(8,128)(2,1)}, bf16[16,16,640]{2,1,0:T(8,128)(2,1)S(1)}, u32[]{:S(2)}, u32[]{:S(2)}) collective-permute-start(bf16[16,16,640]{2,1,0:T(8,128)(2,1)} %all-to-all-done.2), channel_id=1, source_target_pairs={{0,16},{16,0},{1,17},{17,1},{2,18},{18,2},{3,19},{19,3},{4,20},{20... | collective-permute-start | bytes 983048 | tf_op jit(solution)/shard_map/ppermute | solution.py:50
  146.1 6.3 %all-to-all-done.4 = bf16[8,2,32,864]{3,2,1,0:T(8,128)(2,1)S(1)} async-done(((bf16[8,2,32,864]{3,2,1,0:T(8,128)(2,1)}), bf16[8,2,32,864]{3,2,1,0:T(8,128)(2,1)S(1)}, u32[]{:S(2)}, u32[]{:S(2)}) %all-to-all-start.4) | async-done | bytes 884768 | tf_op jit(solution)/shard_map/all_to_all | solution.py:39
  152.9 7.8 %collective-permute-start.5 = (bf16[512,864]{0,1:T(8,128)(2,1)S(1)}, bf16[512,864]{0,1:T(8,128)(2,1)S(1)}, u32[]{:S(2)}, u32[]{:S(2)}) collective-permute-start(bf16[512,864]{0,1:T(8,128)(2,1)S(1)} %copy.16), channel_id=1, source_target_pairs={{0,1},{1,0},{2,3},{3,2},{4,5},{5,4},{6,7},{7,6},{8,9},{9,8},{10,11... | collective-permute-start | bytes 2654216 | tf_op jit(solution)/shard_map/ppermute | solution.py:104
  162.7 1.6 fusion.1
  (49 shorter events, 12.4 us)
Async XLA Ops:
  6.5 78.0 %all-gather.2.cloned.1.call-start = ((), (), s32[]{:S(2)}) async-start(), calls=%async_computation.5 | async-start | bytes 1949696 | tf_op jit(solution)/shard_map/all_gather | solution.py:55
  7.3 8.3 %copy-start.5 = (bf16[32,5120]{1,0:T(8,128)(2,1)S(1)}, bf16[32,5120]{1,0:T(8,128)(2,1)}, u32[]{:S(2)}) copy-start(bf16[32,5120]{1,0:T(8,128)(2,1)} %param.4) | copy-start | bytes 983044
  10.1 54.6 %collective-permute-start = (bf16[944,864]{1,0:T(8,128)(2,1)}, bf16[944,864]{1,0:T(8,128)(2,1)S(1)}, u32[]{:S(2)}, u32[]{:S(2)}) collective-permute-start(bf16[944,864]{1,0:T(8,128)(2,1)} %slice.101), channel_id=1, source_target_pairs={{0,16},{16,0},{1,17},{17,1},{2,18},{18,2},{3,19},{19,3},{4,20},{20... | collective-permute-start | bytes 4893704 | tf_op jit(solution)/shard_map/ppermute | solution.py:50
  17.5 5.1 %copy-start.6 = (bf16[160,320]{1,0:T(8,128)(2,1)S(1)}, bf16[160,320]{1,0:T(8,128)(2,1)}, u32[]{:S(2)}) copy-start(bf16[160,320]{1,0:T(8,128)(2,1)} %param.5) | copy-start | bytes 307204
  17.5 45.0 %all-to-all-start = ((bf16[4,32,1280]{2,1,0:T(8,128)(2,1)}), bf16[4,32,1280]{2,1,0:T(8,128)(2,1)S(1)}, u32[]{:S(2)}, u32[]{:S(2)}) async-start(bf16[4,32,1280]{2,1,0:T(8,128)(2,1)} %reshape.35), calls=%async_computation | async-start | bytes 655360 | tf_op jit(solution)/shard_map/all_to_all | solution.py:60
  64.7 10.5 %all-to-all-start.1 = ((f32[4,32,320]{2,1,0:T(8,128)}), f32[4,32,320]{2,1,0:T(8,128)S(1)}, u32[]{:S(2)}, u32[]{:S(2)}) async-start(f32[4,32,320]{2,1,0:T(8,128)} %fusion.4), calls=%async_computation.1 | async-start | bytes 393216 | tf_op jit(solution)/shard_map/all_to_all | solution.py:67
  69.7 37.5 %collective-permute-start.1 = (bf16[784,864]{1,0:T(8,128)(2,1)S(1)}, bf16[784,864]{1,0:T(8,128)(2,1)}, u32[]{:S(2)}, u32[]{:S(2)}) collective-permute-start(bf16[784,864]{1,0:T(8,128)(2,1)S(1)} %slice.100), channel_id=1, source_target_pairs={{0,16},{16,0},{1,17},{17,1},{2,18},{18,2},{3,19},{19,3},{4,20},{20... | collective-permute-start | bytes 4064264 | tf_op jit(solution)/shard_map/ppermute | solution.py:50
  76.1 31.0 %all-to-all-start.2 = ((bf16[16,16,640]{2,1,0:T(8,128)(2,1)}), bf16[16,16,640]{2,1,0:T(8,128)(2,1)}, u32[]{:S(2)}, u32[]{:S(2)}) async-start(bf16[16,16,640]{2,1,0:T(8,128)(2,1)} %broadcast_in_dim.4), calls=%async_computation.2 | async-start | bytes 655360 | tf_op jit(solution)/shard_map/all_to_all | solution.py:39
  84.6 3.3 %copy-start.4 = (bf16[1728,864]{1,0:T(8,128)(2,1)S(1)}, bf16[1728,864]{1,0:T(8,128)(2,1)}, u32[]{:S(2)}) copy-start(bf16[1728,864]{1,0:T(8,128)(2,1)} %param.7) | copy-start | bytes 8957956
  86.4 2.3 %copy-start = (bf16[256,784]{1,0:T(8,128)(2,1)}, bf16[256,784]{1,0:T(8,128)(2,1)S(1)}, u32[]{:S(2)}) copy-start(bf16[256,784]{1,0:T(8,128)(2,1)S(1)} %get-tuple-element.27) | copy-start | bytes 1204228
  89.5 16.8 %collective-permute-start.2 = (f32[256,864]{0,1:T(8,128)S(1)}, f32[256,864]{0,1:T(8,128)S(1)}, u32[]{:S(2)}, u32[]{:S(2)}) collective-permute-start(f32[256,864]{0,1:T(8,128)S(1)} %convolution_add_fusion), channel_id=1, source_target_pairs={{0,1},{1,0},{2,3},{3,2},{4,5},{5,4},{6,7},{7,6},{8,9},{9,8},{10,11... | collective-permute-start | bytes 2654216 | tf_op jit(solution)/shard_map/ppermute | solution.py:86
  106.3 1.0 copy-start.1
  107.1 2.4 %copy-start.3 = (f32[256,864]{0,1:T(8,128)S(1)}, f32[256,864]{0,1:T(8,128)}, u32[]{:S(2)}) copy-start(f32[256,864]{0,1:T(8,128)} %fusion.19) | copy-start | bytes 2654212
  110.5 4.7 %copy-start.2 = (f32[256,864]{0,1:T(8,128)S(1)}, f32[256,864]{0,1:T(8,128)}, u32[]{:S(2)}) copy-start(f32[256,864]{0,1:T(8,128)} %fusion.20) | copy-start | bytes 2654212
  110.5 4.6 %collective-permute-start.4 = (f32[256,864]{0,1:T(8,128)}, f32[256,864]{0,1:T(8,128)S(1)}, u32[]{:S(2)}, u32[]{:S(2)}) collective-permute-start(f32[256,864]{0,1:T(8,128)} %add.113), channel_id=1, source_target_pairs={{0,1},{1,0},{2,3},{3,2},{4,5},{5,4},{6,7},{7,6},{8,9},{9,8},{10,11... | collective-permute-start | bytes 2654216 | tf_op jit(solution)/shard_map/ppermute | solution.py:86
  138.8 13.5 %all-to-all-start.4 = ((bf16[8,2,32,864]{3,2,1,0:T(8,128)(2,1)}), bf16[8,2,32,864]{3,2,1,0:T(8,128)(2,1)S(1)}, u32[]{:S(2)}, u32[]{:S(2)}) async-start(bf16[8,2,32,864]{3,2,1,0:T(8,128)(2,1)} %broadcast_in_dim.5), calls=%async_computation.4 | async-start | bytes 1835008 | tf_op jit(solution)/shard_map/all_to_all | solution.py:39
  142.4 18.3 %collective-permute-start.3 = (bf16[16,16,640]{2,1,0:T(8,128)(2,1)}, bf16[16,16,640]{2,1,0:T(8,128)(2,1)S(1)}, u32[]{:S(2)}, u32[]{:S(2)}) collective-permute-start(bf16[16,16,640]{2,1,0:T(8,128)(2,1)} %all-to-all-done.2), channel_id=1, source_target_pairs={{0,16},{16,0},{1,17},{17,1},{2,18},{18,2},{3,19},{19,3},{4,20},{20... | collective-permute-start | bytes 983048 | tf_op jit(solution)/shard_map/ppermute | solution.py:50
  152.9 9.9 %collective-permute-start.5 = (bf16[512,864]{0,1:T(8,128)(2,1)S(1)}, bf16[512,864]{0,1:T(8,128)(2,1)S(1)}, u32[]{:S(2)}, u32[]{:S(2)}) collective-permute-start(bf16[512,864]{0,1:T(8,128)(2,1)S(1)} %copy.16), channel_id=1, source_target_pairs={{0,1},{1,0},{2,3},{3,2},{4,5},{5,4},{6,7},{7,6},{8,9},{9,8},{10,11... | collective-permute-start | bytes 2654216 | tf_op jit(solution)/shard_map/ppermute | solution.py:104
Sparse Core Ops, SparseCore 0:
  9.4 75.0 all-gather.1
